TPU v7x, 32 devices: a whole 2x2x4 slice. The times are simulated.
32 devices in a mesh: row: 2 (over y), col: 4 (over z), vec: 4 (over x, core).
Axes of the slice: x: 2, y: 2, z: 4, core: 2. Of those that a mesh axis runs over, the one named last changes fastest.
Arguments:
- particles: bfloat16 [1024, 512], P(('row', 'col', 'vec')), may hold values from -6 to 6
- start_basis: float32 [1024, 64], P(('row', 'col', 'vec')), may hold values from -6 to 6
Outputs:
- basis: float32 [1024, 64], P(('row', 'col', 'vec'))
- factor: float32 [64, 64], replicated
All inputs are finite; a program needn't handle non-finite values.
Results may differ from a plain program's by a relative error of at most 0.0003.
Values may be sent and summed in bfloat16 or wider, within the bound.
No kernel may reach another device: no remote copies, remote signals or barrier semaphores. Data moves between devices by JAX's collectives and lax.ppermute only.
A program may use at most 64 MiB of HBM per device.

v0:
```python
import math

import jax
import jax.numpy as jnp
from jax import lax
from jax.sharding import PartitionSpec as P

ITERS = 2


def local(particles, start_basis):
    shard_rows = particles.shape[0]
    width = particles.shape[1]
    eig_cols = start_basis.shape[1]
    row_size = lax.axis_size("row")
    col_size = lax.axis_size("col")
    vec_size = lax.axis_size("vec")
    total_rows = shard_rows * row_size * col_size * vec_size
    rowpos = lax.axis_index("row")
    colpos = lax.axis_index("col")
    vecpos = lax.axis_index("vec")
    spread = 2.0 * width
    root_total = math.sqrt(float(total_rows))
    row_feats = lax.all_gather(particles, "row", axis=0, tiled=True)
    col_feats = lax.all_gather(particles, ("col", "vec"), axis=0, tiled=True)
    row_iota = jnp.arange(row_feats.shape[0], dtype=jnp.int32)
    col_iota = jnp.arange(col_feats.shape[0], dtype=jnp.int32)
    row_ids = (
        (row_iota // shard_rows * col_size + colpos) * vec_size + vecpos
    ) * shard_rows + row_iota % shard_rows
    col_ids = (
        (rowpos * col_size + col_iota // (vec_size * shard_rows)) * vec_size
        + col_iota // shard_rows % vec_size
    ) * shard_rows + col_iota % shard_rows
    row_sq = jnp.sum(jnp.square(row_feats.astype(jnp.float32)), axis=1)
    col_sq = jnp.sum(jnp.square(col_feats.astype(jnp.float32)), axis=1)
    same_particle = row_ids[:, None] == col_ids[None, :]

    def make_tile():
        inner_dots = lax.dot_general(
            row_feats, col_feats, (((1,), (1,)), ((), ())), preferred_element_type=jnp.float32
        )
        distance = row_sq[:, None] + col_sq[None, :] - 2.0 * inner_dots
        return jnp.where(same_particle, jnp.float32(0.0), jnp.exp(-distance / spread))

    kernel_tile = make_tile()
    row_degree = jnp.sum(kernel_tile, axis=1)
    degree = lax.psum_scatter(row_degree, "row", scatter_dimension=0, tiled=True)
    root_deg = jnp.sqrt(degree)
    inv_root = 1.0 / root_deg
    local_total = jnp.sum(degree)
    degree_sum, raw_align = lax.psum(
        (local_total, jnp.dot(root_deg, start_basis, precision=lax.Precision.HIGHEST)),
        ("row", "col", "vec"),
    )
    aligned = raw_align / jnp.sqrt(degree_sum)
    basis_now = start_basis
    factor = jnp.zeros((eig_cols, eig_cols), jnp.float32)
    for sweep in range(ITERS):
        current = make_tile()
        scaled = basis_now * inv_root[:, None]
        partial_prod = jnp.dot(
            current,
            lax.all_gather(scaled, ("col", "vec"), axis=0, tiled=True),
            precision=lax.Precision.HIGHEST,
        )
        product = lax.psum_scatter(partial_prod, "row", scatter_dimension=0, tiled=True)
        weighted = product * inv_root[:, None]
        root_vec = root_deg / jnp.sqrt(degree_sum)
        deflated = weighted - root_vec[:, None] * aligned[None, :]
        gram_mat, tail = lax.psum(
            (
                jnp.dot(deflated.T, deflated, precision=lax.Precision.HIGHEST),
                jnp.dot(root_vec, deflated, precision=lax.Precision.HIGHEST),
            ),
            ("row", "col", "vec"),
        )
        factor = jnp.linalg.cholesky(gram_mat)
        aligned = root_total * jax.scipy.linalg.solve_triangular(factor, tail, lower=True)
        solved = jax.scipy.linalg.solve_triangular(factor, deflated.T, lower=True)
        basis_now = solved.T * root_total
    return (basis_now, factor)


def solution(mesh):
    placed = (P(("row", "col", "vec"), None), P(("row", "col", "vec"), None))
    return jax.shard_map(
        local,
        mesh=mesh,
        in_specs=placed,
        out_specs=(P(("row", "col", "vec"), None), P()),
        check_vma=False,
    )
```

profile of v0, /device:TPU:0, one launch (start us, length us, event | category | flops | bytes accessed | tf_op | source)
XLA Modules:
  0.0 249.2 jit_solution(3311690041121054222)
XLA Ops:
  7.2 0.0 reduce-scatter.3.cloned.1.call-start
  7.2 0.0 copy-start
  7.2 24.8 %all_gather.13 = bf16[512,512]{1,0:T(8,128)(2,1)S(1)} all-gather(bf16[32,512]{1,0:T(8,128)(2,1)} %param.5), channel_id=1, replica_groups=mesh['row'=2,'col'=4,'vec'=4] {'col','vec'}, dimensions={0}, use_global_device_ids=true | all-gather | bytes 557056 | tf_op jit(solution)/shard_map/all_gather | solution.py:25
  32.0 0.0 copy-done
  32.0 4.6 %all_gather.12 = bf16[64,512]{1,0:T(8,128)(2,1)S(1)} all-gather(bf16[32,512]{1,0:T(8,128)(2,1)S(1)} %copy-done), channel_id=1, replica_groups=mesh['row'=2,'col'=4,'vec'=4] {'row'}, dimensions={0}, use_global_device_ids=true | all-gather | bytes 98304 | tf_op jit(solution)/shard_map/all_gather | solution.py:24
  36.6 0.2 multiply_reduce_fusion
  36.8 0.1 multiply_reduce_fusion.1
  36.9 0.4 fusion.59
  37.3 0.0 copy-start.1
  37.3 4.9 %all-reduce = f32[64]{0:T(128)S(1)} all-reduce(f32[64]{0:T(128)S(1)} %get-tuple-element.13), channel_id=2, replica_groups=mesh['row'=2,'col'=4,'vec'=4] {'row'}, use_global_device_ids=true, to_apply=%region_3.4.clone | all-reduce | flops 64 | bytes 512
  42.3 0.0 copy-start.4
  42.3 0.7 copy-done.4
  42.9 0.6 dynamic-slice
  44.2 0.1 broadcast_multiply_fusion.1
  44.2 0.0 copy-done.1
  44.2 0.1 broadcast_multiply_fusion
  44.3 17.8 %all_gather.14 = f32[512,64]{1,0:T(8,128)S(1)} all-gather(f32[32,64]{1,0:T(8,128)S(1)} %broadcast_multiply_fusion), channel_id=1, replica_groups=mesh['row'=2,'col'=4,'vec'=4] {'col','vec'}, dimensions={0}, use_global_device_ids=true | all-gather | bytes 139264 | tf_op jit(solution)/shard_map/all_gather | solution.py:64
  62.2 0.9 fusion.60
  63.1 0.0 reduce-scatter.3.cloned.1.call-update
  63.1 0.0 reduce-scatter.5.cloned.1.call-start
  63.1 0.1 convolution_bitcast_fusion.2
  63.3 0.6 reduce_sum.39
  63.9 38.7 %all-reduce.2 = (f32[64]{0:T(128)S(1)}, f32[]{:T(128)}) all-reduce(f32[64]{0:T(128)S(1)} %convolution_bitcast_fusion.2, f32[]{:T(128)} %reduce_sum.39), channel_id=1, replica_groups=mesh['row'=2,'col'=4,'vec'=4] {'row','col','vec'}, use_global_device_ids=true, to_apply=%region_7.8 | all-reduce | flops 65 | bytes 520 | tf_op jit(solution)/shard_map/psum | solution.py:52
  103.3 0.0 reduce-scatter.3.cloned.1.call-done
  103.3 0.0 copy-start.2
  103.3 1.0 convolution_bitcast_fusion.1
  104.3 0.0 copy-done.2
  104.3 0.3 fusion.20
  104.6 41.9 %all-reduce.1 = (f32[64,64]{0,1:T(8,128)S(1)}, f32[64]{0:T(128)S(1)}) all-reduce(f32[64,64]{0,1:T(8,128)S(1)} %fusion.20, f32[64]{0:T(128)S(1)} %convolution_bitcast_fusion.1), channel_id=1, replica_groups=mesh['row'=2,'col'=4,'vec'=4] {'row','col','vec'}, use_global_device_ids=true, to_apply=%region_8.9 | all-reduce | flops 4160 | bytes 33280 | tf_op jit(solution)/shard_map/psum | solution.py:71
  146.5 0.1 copy.9
  146.6 5.8 %cholesky.44 = f32[64,64]{1,0:T(8,128)S(1)} custom-call(f32[64,64]{1,0:T(8,128)S(1)} %fusion.13), custom_call_target="Cholesky" | custom-call | tf_op jit(solution)/shard_map/jit(cholesky)/cholesky | solution.py:78
  152.5 0.6 compare_reduce_fusion.1
  153.1 0.7 fusion.8
  153.8 4.9 %custom-call.11 = f32[1,64,64]{1,2,0:T(8,128)S(1)} custom-call(f32[1,64,64]{2,1,0:T(8,128)S(1)} %fusion.8), custom_call_target="InvertDiagBlocksLowerTriangular" | custom-call | tf_op jit(solution)/shard_map/jit(_solve_triangular)/triangular_solve | solution.py:80
  158.7 0.2 fusion.6
  158.9 21.1 %all_gather.15 = f32[512,64]{1,0:T(8,128)S(1)} all-gather(f32[32,64]{1,0:T(8,128)S(1)} %fusion.6), channel_id=1, replica_groups=mesh['row'=2,'col'=4,'vec'=4] {'col','vec'}, dimensions={0}, use_global_device_ids=true | all-gather | bytes 139264 | tf_op jit(solution)/shard_map/all_gather | solution.py:64
  180.0 0.9 fusion.61
  180.9 0.0 reduce-scatter.5.cloned.1.call-update
  180.9 0.1 fusion.7
  181.0 7.1 %reduce-scatter.5.cloned.1.call-done = f32[32,64]{1,0:T(8,128)} async-done(((f32[64,64]{1,0:T(8,128)}), f32[32,64]{1,0:T(8,128)}) %reduce-scatter.5.cloned.1.call-update) | async-done | bytes 8208 | tf_op jit(solution)/shard_map/reduce_scatter | solution.py:67
  188.1 1.1 fusion.19
  189.3 39.5 %psum.39 = f32[64,64]{0,1:T(8,128)S(1)} all-reduce(f32[64,64]{0,1:T(8,128)S(1)} %fusion.19), channel_id=1, replica_groups=mesh['row'=2,'col'=4,'vec'=4] {'row','col','vec'}, use_global_device_ids=true, to_apply=%region_13.16 | all-reduce | flops 4096 | bytes 32768 | tf_op jit(solution)/shard_map/psum | solution.py:71
  228.7 0.1 copy.11
  228.8 5.8 %cholesky.55 = f32[64,64]{1,0:T(8,128)S(1)} custom-call(f32[64,64]{1,0:T(8,128)S(1)} %fusion.10), custom_call_target="Cholesky" | custom-call | tf_op jit(solution)/shard_map/jit(cholesky)/cholesky | solution.py:78
  234.7 0.6 compare_reduce_fusion
  235.4 0.0 copy-start.3
  235.4 1.3 select_bitcast_fusion
  236.7 4.9 %custom-call.12 = f32[1,64,64]{1,2,0:T(8,128)S(1)} custom-call(f32[1,64,64]{2,1,0:T(8,128)S(1)} %get-tuple-element.8), custom_call_target="InvertDiagBlocksLowerTriangular" | custom-call | tf_op jit(solution)/shard_map/jit(_solve_triangular)/triangular_solve | solution.py:80
  241.5 0.0 copy-done.3
  241.6 0.8 fusion.5
  (8 shorter events, 0.1 us)
Async XLA Ops:
  7.2 96.1 %reduce-scatter.3.cloned.1.call-start = ((), (), s32[]{:S(2)}) async-start(), calls=%async_computation.2 | async-start | bytes 49152 | tf_op jit(solution)/shard_map/reduce_scatter | solution.py:67
  7.2 24.8 %copy-start = (bf16[32,512]{1,0:T(8,128)(2,1)S(1)}, bf16[32,512]{1,0:T(8,128)(2,1)}, u32[]{:S(2)}) copy-start(bf16[32,512]{1,0:T(8,128)(2,1)} %param.5) | copy-start | bytes 98308
  37.3 6.9 %copy-start.1 = (f32[32,64]{1,0:T(8,128)S(1)}, f32[32,64]{1,0:T(8,128)}, u32[]{:S(2)}) copy-start(f32[32,64]{1,0:T(8,128)} %param.6) | copy-start | bytes 24580
  42.3 0.7 copy-start.4
  63.1 125.1 %reduce-scatter.5.cloned.1.call-start = ((), (), s32[]{:S(2)}) async-start(), calls=%async_computation.3 | async-start | bytes 49152 | tf_op jit(solution)/shard_map/reduce_scatter | solution.py:67
  103.3 1.0 copy-start.2
  235.4 6.2 %copy-start.3 = (f32[32,64]{1,0:T(8,128)S(1)}, f32[32,64]{1,0:T(8,128)}, u32[]{:S(2)}) copy-start(f32[32,64]{1,0:T(8,128)} %reduce-scatter.5.cloned.1.call-done) | copy-start | bytes 24580
Sparse Core Ops, SparseCore 0:
  63.2 8.8 reduce-scatter.2
  181.0 7.0 reduce-scatter.4
where the time goes:
time: 250 us; the launch traced here: 249 us
  blocking collectives  193 us (77%)
  other arithmetic  25.9 us (10%)
  between operations  15.5 us (6%)
  waiting for transfers between devices  7.17 us (3%)
  matrix products  5.91 us (2%)
    psum x2, blocking collectives, local(): lax.psum((jnp.dot(deflated.T, deflated, precision=lax.Precision.HIGHEST),...  81.4 us
    all_gather x2, blocking collectives, local(): lax.all_gather(scaled, ('col', 'vec'), axis=0, tiled=True)  38.9 us
    psum x1, blocking collectives, local(): lax.psum((local_total, jnp.dot(root_deg, start_basis, precision=lax.Preci...  38.7 us
    all_gather x1, blocking collectives, local(): col_feats = lax.all_gather(particles, ('col', 'vec'), axis=0, tiled=True)  24.8 us
    another operation x6, other arithmetic, local(): factor = jnp.linalg.cholesky(gram_mat)  13 us
    another operation x4, other arithmetic, local(): solved = jax.scipy.linalg.solve_triangular(factor, deflated.T, lower=True)  11.7 us
    reduce_scatter x2, waiting for transfers between devices, local(): lax.psum_scatter(partial_prod, 'row', scatter_dimension=0, tiled=True)  7.13 us
  transfers between devices with their start and end apart: 2, of which 1 were waited for; matrix products, arithmetic and copies ran while one was open for 0% of the time, Pallas kernels for 0%

commit v1 on v0

--- a/solution.py
+++ b/solution.py
@@ -6,9 +6,11 @@
 from jax.sharding import PartitionSpec as P
 
 ITERS = 2
+AXES = ("row", "col", "vec")
+WHOLE_ROWS = 2048
 
 
-def local(particles, start_basis):
+def sharded(particles, start_basis):
     shard_rows = particles.shape[0]
     width = particles.shape[1]
     eig_cols = start_basis.shape[1]
@@ -35,32 +37,26 @@
     row_sq = jnp.sum(jnp.square(row_feats.astype(jnp.float32)), axis=1)
     col_sq = jnp.sum(jnp.square(col_feats.astype(jnp.float32)), axis=1)
     same_particle = row_ids[:, None] == col_ids[None, :]
-
-    def make_tile():
-        inner_dots = lax.dot_general(
-            row_feats, col_feats, (((1,), (1,)), ((), ())), preferred_element_type=jnp.float32
-        )
-        distance = row_sq[:, None] + col_sq[None, :] - 2.0 * inner_dots
-        return jnp.where(same_particle, jnp.float32(0.0), jnp.exp(-distance / spread))
-
-    kernel_tile = make_tile()
+    inner_dots = lax.dot_general(
+        row_feats, col_feats, (((1,), (1,)), ((), ())), preferred_element_type=jnp.float32
+    )
+    distance = row_sq[:, None] + col_sq[None, :] - 2.0 * inner_dots
+    kernel_tile = jnp.where(same_particle, jnp.float32(0.0), jnp.exp(-distance / spread))
     row_degree = jnp.sum(kernel_tile, axis=1)
     degree = lax.psum_scatter(row_degree, "row", scatter_dimension=0, tiled=True)
     root_deg = jnp.sqrt(degree)
     inv_root = 1.0 / root_deg
     local_total = jnp.sum(degree)
     degree_sum, raw_align = lax.psum(
-        (local_total, jnp.dot(root_deg, start_basis, precision=lax.Precision.HIGHEST)),
-        ("row", "col", "vec"),
+        (local_total, jnp.dot(root_deg, start_basis, precision=lax.Precision.HIGHEST)), AXES
     )
     aligned = raw_align / jnp.sqrt(degree_sum)
     basis_now = start_basis
     factor = jnp.zeros((eig_cols, eig_cols), jnp.float32)
     for sweep in range(ITERS):
-        current = make_tile()
         scaled = basis_now * inv_root[:, None]
         partial_prod = jnp.dot(
-            current,
+            kernel_tile,
             lax.all_gather(scaled, ("col", "vec"), axis=0, tiled=True),
             precision=lax.Precision.HIGHEST,
         )
@@ -73,7 +69,7 @@
                 jnp.dot(deflated.T, deflated, precision=lax.Precision.HIGHEST),
                 jnp.dot(root_vec, deflated, precision=lax.Precision.HIGHEST),
             ),
-            ("row", "col", "vec"),
+            AXES,
         )
         factor = jnp.linalg.cholesky(gram_mat)
         aligned = root_total * jax.scipy.linalg.solve_triangular(factor, tail, lower=True)
@@ -82,12 +78,66 @@
     return (basis_now, factor)
 
 
+def replicated(particles, start_basis):
+    shard_rows, width = particles.shape
+    eig_cols = start_basis.shape[1]
+    base_hi = lax.reduce_precision(start_basis, 8, 7)
+    rest = start_basis - base_hi
+    base_mid = lax.reduce_precision(rest, 8, 7)
+    base_hi, base_mid, base_lo = (
+        part.astype(jnp.bfloat16) for part in (base_hi, base_mid, rest - base_mid)
+    )
+    packed = jnp.concatenate([particles, base_hi, base_mid, base_lo, jnp.zeros_like(base_lo)], axis=1)
+    everything = lax.all_gather(packed, AXES, axis=0, tiled=True)
+    feats = everything[:, :width]
+    basis = (
+        everything[:, width : width + eig_cols].astype(jnp.float32)
+        + everything[:, width + eig_cols : width + 2 * eig_cols].astype(jnp.float32)
+        + everything[:, width + 2 * eig_cols : width + 3 * eig_cols].astype(jnp.float32)
+    )
+    total_rows = feats.shape[0]
+    spread = 2.0 * width
+    root_total = math.sqrt(float(total_rows))
+    place = (lax.axis_index("row") * lax.axis_size("col") + lax.axis_index("col")) * lax.axis_size(
+        "vec"
+    ) + lax.axis_index("vec")
+    squares = jnp.sum(jnp.square(feats.astype(jnp.float32)), axis=1)
+    inner_dots = lax.dot_general(
+        feats, feats, (((1,), (1,)), ((), ())), preferred_element_type=jnp.float32
+    )
+    distance = squares[:, None] + squares[None, :] - 2.0 * inner_dots
+    ids = jnp.arange(total_rows, dtype=jnp.int32)
+    kernel = jnp.where(ids[:, None] == ids[None, :], jnp.float32(0.0), jnp.exp(-distance / spread))
+    degree = jnp.sum(kernel, axis=1)
+    root_deg = jnp.sqrt(degree)
+    inv_root = 1.0 / root_deg
+    root_vec = root_deg / jnp.sqrt(jnp.sum(degree))
+    matrix = kernel * inv_root[:, None] * inv_root[None, :] - root_vec[:, None] * root_vec[None, :]
+    now = basis
+    factor = None
+    for sweep in range(ITERS):
+        now = jnp.dot(matrix, now, precision=lax.Precision.HIGHEST)
+        gram = jnp.dot(now.T, now, precision=lax.Precision.HIGHEST)
+        factor = jnp.linalg.cholesky(gram)
+        if sweep == ITERS - 1:
+            now = lax.dynamic_slice_in_dim(now, place * shard_rows, shard_rows, 0)
+        now = jax.scipy.linalg.solve_triangular(factor, now.T, lower=True).T * root_total
+    return (now, factor)
+
+
+def local(particles, start_basis):
+    devices = lax.axis_size("row") * lax.axis_size("col") * lax.axis_size("vec")
+    if particles.shape[0] * devices <= WHOLE_ROWS:
+        return replicated(particles, start_basis)
+    return sharded(particles, start_basis)
+
+
 def solution(mesh):
-    placed = (P(("row", "col", "vec"), None), P(("row", "col", "vec"), None))
+    placed = (P(AXES, None), P(AXES, None))
     return jax.shard_map(
         local,
         mesh=mesh,
         in_specs=placed,
-        out_specs=(P(("row", "col", "vec"), None), P()),
+        out_specs=(P(AXES, None), P()),
         check_vma=False,
     )

time: 250 us -> 123 us (0.49)
  blocking collectives: 193 us -> 0 us
  waiting for transfers between devices: 7.17 us -> 59.1 us
  matrix products: 5.91 us -> 20.4 us
    psum x3 -> x0, blocking collectives: 120 us -> none  [the longest x2 81.4 us: local(): lax.psum((jnp.dot(deflated.T, deflated, precision=lax.Precision.HIGHEST),...]
    all_gather x4 -> x0, blocking collectives: 68.3 us -> none  [the longest x2 38.9 us: local(): lax.all_gather(scaled, ('col', 'vec'), axis=0, tiled=True)]
    all_gather x0 -> x1, waiting for transfers between devices: none -> 59.1 us  [replicated(): everything = lax.all_gather(packed, AXES, axis=0, tiled=True)]
    dot_general x7 -> x5, matrix products: 4.72 us -> 18.5 us  [the longest x2 11.7 us: replicated(): now = jnp.dot(matrix, now, precision=lax.Precision.HIGHEST)]
    reduce_scatter x2 -> x0, waiting for transfers between devices: 7.13 us -> none  [local(): lax.psum_scatter(partial_prod, 'row', scatter_dimension=0, tiled=True)]
    unnamed x1 -> x0, blocking collectives: 4.94 us -> none
  transfers between devices with their start and end apart: 2 -> 1, of which waited for: 1 -> 1; matrix products, arithmetic and copies ran while one was open for 0% -> 0% of each run, Pallas kernels for 0% -> 0%
where the time goes in v1:
time: 123 us
  waiting for transfers between devices  59.1 us (48%)
  other arithmetic  27 us (22%)
  matrix products  20.4 us (17%)
  between operations  14.8 us (12%)
  local copies, waits for them, and re-layouts  1.61 us (1%)
    all_gather x1, waiting for transfers between devices, replicated(): everything = lax.all_gather(packed, AXES, axis=0, tiled=True)  59.1 us
    another operation x6, other arithmetic, replicated(): factor = jnp.linalg.cholesky(gram)  13 us
    dot_general x2, matrix products, replicated(): now = jnp.dot(matrix, now, precision=lax.Precision.HIGHEST)  11.7 us
    another operation x4, other arithmetic, replicated(): jax.scipy.linalg.solve_triangular(factor, now.T, lower=True).T * root_total  11.7 us
    dot_general x1, matrix products, replicated(): lax.dot_general(feats, feats, (((1,), (1,)), ((), ())), preferred_element...  6.04 us
  transfers between devices with their start and end apart: 1, of which 1 were waited for; matrix products, arithmetic and copies ran while one was open for 0% of the time, Pallas kernels for 0%

profile of v1, /device:TPU:0, one launch (start us, length us, event | category | flops | bytes accessed | tf_op | source)
XLA Modules:
  0.0 123.0 jit_solution(9625848818199077032)
XLA Ops:
  7.2 0.0 all-gather.2.cloned.1.call-start
  7.2 0.7 fusion.25
  7.9 1.5 %concatenate.3 = bf16[32,768]{1,0:T(8,128)(2,1)} concatenate(bf16[32,512]{1,0:T(8,128)(2,1)} %param.3, bf16[32,64]{1,0:T(8,128)(2,1)S(1)} %get-tuple-element.9, bf16[32,64]{1,0:T(8,128)(2,1)S(1)} %get-tuple-element.8, bf16[32,64]{1,0:T(8,128)(2,1)S(1)} %get-tuple-element.7, bf16[32,64]{1,0:T(8,128)(2,1)S(1)} %broadcast_in_dim.7), dimensions={1} | concatenate | bytes 98304 | tf_op jit(solution)/shard_map/concatenate | solution.py:90
  9.4 0.0 all-gather.2.cloned.1.call-update
  9.4 59.1 %all-gather.2.cloned.1.call-done = bf16[1024,768]{1,0:T(8,128)(2,1)} async-done(((bf16[32,768]{1,0:T(8,128)(2,1)}), bf16[1024,768]{1,0:T(8,128)(2,1)}) %all-gather.2.cloned.1.call-update) | async-done | bytes 1572880 | tf_op jit(solution)/shard_map/all_gather | solution.py:91
  68.6 1.5 %multiply_reduce_fusion = f32[1024]{0:T(1024)S(1)} fusion(bf16[1024,768]{1,0:T(8,128)(2,1)} %all-gather.2.cloned.1.call-done), kind=kLoop, calls=%fused_computation.13 | loop fusion | flops 1571840 | bytes 1052672 | tf_op jit(solution)/shard_map/reduce_sum | solution.py:104
  70.1 6.0 %fusion.27 = (f32[]{:T(128)}, f32[1024]{0:T(1024)S(1)}, f32[1024,1024]{0,1:T(8,128)}) fusion(bf16[1024,768]{1,0:T(8,128)(2,1)} %all-gather.2.cloned.1.call-done, f32[1024]{0:T(1024)S(1)} %multiply_reduce_fusion), kind=kOutput, calls=%fused_computation.49 | convolution fusion | flops 1083177984 | bytes 5255172 | tf_op jit(solution)/shard_map/dot_general | solution.py:105
  76.8 5.9 %fusion.1 = f32[1024,64]{0,1:T(8,128)S(1)} fusion(f32[1024,1024]{0,1:T(8,128)} %get-tuple-element.12, f32[1024]{0:T(1024)S(1)} %get-tuple-element.11, f32[1024]{0:T(1024)S(1)} %get-tuple-element.10, bf16[1024,768]{1,0:T(8,128)(2,1)} %all-gather.2.cloned.1.call-done), kind=kOutput, calls=%fused_computation.4 | convolution fusion | flops 809828352 | bytes 5259264 | tf_op jit(solution)/shard_map/dot_general | solution.py:119
  82.7 0.4 fusion.29
  83.1 0.1 copy.4
  83.2 5.8 %cholesky.44 = f32[64,64]{1,0:T(8,128)S(1)} custom-call(f32[64,64]{1,0:T(8,128)S(1)} %fusion.23), custom_call_target="Cholesky" | custom-call | tf_op jit(solution)/shard_map/jit(cholesky)/cholesky | solution.py:121
  89.1 0.6 compare_reduce_fusion.1
  89.7 0.7 fusion.19
  90.4 4.9 %custom-call.10 = f32[1,64,64]{1,2,0:T(8,128)S(1)} custom-call(f32[1,64,64]{2,1,0:T(8,128)S(1)} %fusion.19), custom_call_target="InvertDiagBlocksLowerTriangular" | custom-call | tf_op jit(solution)/shard_map/jit(_solve_triangular)/triangular_solve | solution.py:124
  95.3 1.0 convolution_multiply_fusion
  96.3 5.8 %fusion = f32[1024,64]{0,1:T(8,128)S(1)} fusion(f32[1024,64]{1,0:T(8,128)S(1)} %convolution_multiply_fusion, f32[1024,1024]{0,1:T(8,128)} %get-tuple-element.12, f32[1024]{0:T(1024)S(1)} %get-tuple-element.11, f32[1024]{0:T(1024)S(1)} %get-tuple-element.10), kind=kOutput, calls=%fused_computation.3 | convolution fusion | flops 809500672 | bytes 4726784 | tf_op jit(solution)/shard_map/dot_general | solution.py:119
  102.1 0.4 fusion.30
  102.5 0.1 copy.5
  102.6 5.8 %cholesky.55 = f32[64,64]{1,0:T(8,128)S(1)} custom-call(f32[64,64]{1,0:T(8,128)S(1)} %fusion.21), custom_call_target="Cholesky" | custom-call | tf_op jit(solution)/shard_map/jit(cholesky)/cholesky | solution.py:121
  108.5 0.6 compare_reduce_fusion
  109.1 1.3 %select_bitcast_fusion = (f32[1,64,64]{2,1,0:T(8,128)S(1)}, f32[64,64]{1,0:T(8,128)}) fusion(f32[64,64]{1,0:T(8,128)S(1)} %cholesky.55, pred[]{:T(512)} %compare_reduce_fusion), kind=kLoop, calls=%fused_computation.37 | loop fusion | flops 16384 | bytes 49153 | tf_op jit(solution)/shard_map/jit(_solve_triangular)/triangular_solve | solution.py:124
  110.4 4.9 %custom-call.11 = f32[1,64,64]{1,2,0:T(8,128)S(1)} custom-call(f32[1,64,64]{2,1,0:T(8,128)S(1)} %get-tuple-element.5), custom_call_target="InvertDiagBlocksLowerTriangular" | custom-call | tf_op jit(solution)/shard_map/jit(_solve_triangular)/triangular_solve | solution.py:124
  115.3 0.9 convolution_multiply_fusion.1
  (6 shorter events, 0.1 us)
Async XLA Ops:
  7.2 61.4 %all-gather.2.cloned.1.call-start = ((), (), s32[]{:S(2)}) async-start(), calls=%async_computation | async-start | bytes 1622016 | tf_op jit(solution)/shard_map/all_gather | solution.py:91
Sparse Core Ops, SparseCore 0:
  10.9 57.6 all-gather.1

commit v2 on v1

--- a/solution.py
+++ b/solution.py
@@ -78,29 +78,38 @@
     return (basis_now, factor)
 
 
+def swap(block, axis_sizes, bits):
+    count = math.prod(axis_sizes)
+    return lax.ppermute(block, AXES, [(place, place ^ bits) for place in range(count)])
+
+
+def gather_all(block):
+    sizes = tuple(lax.axis_size(name) for name in AXES)
+    vec_size = sizes[2]
+    col_bits = [k * vec_size for k in range(1, sizes[1])]
+    row_bit = sizes[1] * vec_size
+    plane_bits = [r * row_bit + v for r in range(sizes[0]) for v in range(0, vec_size, 2)][1:]
+    for bits in (col_bits, plane_bits, [1]):
+        block = jnp.concatenate([block] + [swap(block, sizes, k) for k in bits], axis=0)
+    return block
+
+
 def replicated(particles, start_basis):
     shard_rows, width = particles.shape
     eig_cols = start_basis.shape[1]
     base_hi = lax.reduce_precision(start_basis, 8, 7)
-    rest = start_basis - base_hi
-    base_mid = lax.reduce_precision(rest, 8, 7)
-    base_hi, base_mid, base_lo = (
-        part.astype(jnp.bfloat16) for part in (base_hi, base_mid, rest - base_mid)
+    base_lo = lax.reduce_precision(start_basis - base_hi, 8, 7)
+    packed = jnp.concatenate(
+        [particles, base_hi.astype(jnp.bfloat16), base_lo.astype(jnp.bfloat16)], axis=1
     )
-    packed = jnp.concatenate([particles, base_hi, base_mid, base_lo, jnp.zeros_like(base_lo)], axis=1)
-    everything = lax.all_gather(packed, AXES, axis=0, tiled=True)
+    everything = gather_all(packed)
     feats = everything[:, :width]
-    basis = (
-        everything[:, width : width + eig_cols].astype(jnp.float32)
-        + everything[:, width + eig_cols : width + 2 * eig_cols].astype(jnp.float32)
-        + everything[:, width + 2 * eig_cols : width + 3 * eig_cols].astype(jnp.float32)
-    )
+    basis = everything[:, width : width + eig_cols].astype(jnp.float32) + everything[
+        :, width + eig_cols : width + 2 * eig_cols
+    ].astype(jnp.float32)
     total_rows = feats.shape[0]
     spread = 2.0 * width
     root_total = math.sqrt(float(total_rows))
-    place = (lax.axis_index("row") * lax.axis_size("col") + lax.axis_index("col")) * lax.axis_size(
-        "vec"
-    ) + lax.axis_index("vec")
     squares = jnp.sum(jnp.square(feats.astype(jnp.float32)), axis=1)
     inner_dots = lax.dot_general(
         feats, feats, (((1,), (1,)), ((), ())), preferred_element_type=jnp.float32
@@ -120,7 +129,7 @@
         gram = jnp.dot(now.T, now, precision=lax.Precision.HIGHEST)
         factor = jnp.linalg.cholesky(gram)
         if sweep == ITERS - 1:
-            now = lax.dynamic_slice_in_dim(now, place * shard_rows, shard_rows, 0)
+            now = now[:shard_rows]
         now = jax.scipy.linalg.solve_triangular(factor, now.T, lower=True).T * root_total
     return (now, factor)
 

time: 123 us -> 69.3 us (0.56)
  waiting for transfers between devices: 59.1 us -> 11.8 us
  between operations: 14.8 us -> 1.47 us
  starting transfers between devices: 0.04 us -> 9.26 us
  matrix products: 20.4 us -> 18.5 us
    all_gather x1 -> x0, waiting for transfers between devices: 59.1 us -> none  [replicated(): everything = lax.all_gather(packed, AXES, axis=0, tiled=True)]
    ppermute x0 -> x7, waiting for transfers between devices: none -> 11.8 us  [swap(): lax.ppermute(block, AXES, [(place, place ^ bits) for place in range(count)])]
    ppermute x0 -> x7, starting transfers between devices: none -> 9.26 us  [swap(): lax.ppermute(block, AXES, [(place, place ^ bits) for place in range(count)])]
    dot_general x1, matrix products: 6.04 us -> 4.45 us  [replicated(): lax.dot_general(feats, feats, (((1,), (1,)), ((), ())), preferred_element...]
    concatenate x1 -> x2, local copies, waits for them, and re-layouts: 1.46 us -> 0.14 us  [gather_all(): jnp.concatenate([block] + [swap(block, sizes, k) for k in bits], axis=0)]
  transfers between devices with their start and end apart: 1 -> 7, of which waited for: 1 -> 4; matrix products, arithmetic and copies ran while one was open for 0% -> 0% of each run, Pallas kernels for 0% -> 0%
where the time goes in v2:
time: 69.3 us; the launch traced here: 68.8 us
  other arithmetic  27.4 us (40%)
  matrix products  18.5 us (27%)
  waiting for transfers between devices  11.8 us (17%)
  starting transfers between devices  9.26 us (13%)
  between operations  1.47 us (2%)
    another operation x6, other arithmetic, replicated(): factor = jnp.linalg.cholesky(gram)  13 us
    ppermute x7, waiting for transfers between devices, swap(): lax.ppermute(block, AXES, [(place, place ^ bits) for place in range(count)])  11.8 us
    another operation x4, other arithmetic, replicated(): jax.scipy.linalg.solve_triangular(factor, now.T, lower=True).T * root_total  11.7 us
    dot_general x2, matrix products, replicated(): now = jnp.dot(matrix, now, precision=lax.Precision.HIGHEST)  11.4 us
    ppermute x7, starting transfers between devices, swap(): lax.ppermute(block, AXES, [(place, place ^ bits) for place in range(count)])  9.26 us
    dot_general x1, matrix products, replicated(): lax.dot_general(feats, feats, (((1,), (1,)), ((), ())), preferred_element...  4.45 us
    another operation x2, matrix products, replicated(): jax.scipy.linalg.solve_triangular(factor, now.T, lower=True).T * root_total  1.87 us
  transfers between devices with their start and end apart: 7, of which 4 were waited for; matrix products, arithmetic and copies ran while one was open for 0% of the time, Pallas kernels for 0%

profile of v2, /device:TPU:0, one launch (start us, length us, event | category | flops | bytes accessed | tf_op | source)
XLA Modules:
  0.0 68.8 jit_solution(11748912314224092324)
XLA Ops:
  0.6 0.7 %reduce-precision_convert_fusion = (bf16[32,64]{1,0:T(8,128)(2,1)S(1)}, bf16[32,64]{1,0:T(8,128)(2,1)S(1)}) fusion(f32[32,64]{1,0:T(8,128)} %param.4), kind=kLoop, calls=%fused_computation.55 | loop fusion | flops 10240 | bytes 16384 | tf_op jit(solution)/shard_map/convert_element_type | solution.py:103
  1.4 0.8 %constant_dynamic-update-slice_fusion.6 = (bf16[512,640]{1,0:T(8,128)(2,1)S(1)}, bf16[32,640]{1,0:T(8,128)(2,1)S(1)}) fusion(bf16[32,64]{1,0:T(8,128)(2,1)S(1)} %get-tuple-element.22, bf16[32,64]{1,0:T(8,128)(2,1)S(1)} %get-tuple-element.21, bf16[32,512]{1,0:T(8,128)(2,1)} %param.3), kind=kLoop, calls=%fused_computation.33 | loop fusion | flops 122879 | bytes 122880
  2.2 5.1 %collective-permute-start.2 = (bf16[32,640]{1,0:T(8,128)(2,1)S(1)}, bf16[32,640]{1,0:T(8,128)(2,1)S(1)}, u32[]{:S(2)}, u32[]{:S(2)}) collective-permute-start(bf16[32,640]{1,0:T(8,128)(2,1)S(1)} %get-tuple-element.8), channel_id=1, source_target_pairs={{0,12},{1,13},{2,14},{3,15},{4,8},{5,9},{6,10},{7,11},{8,4},{9,5},... | collective-permute-start | bytes 122888 | tf_op jit(solution)/shard_map/ppermute | solution.py:83
  7.2 0.0 collective-permute-start.1
  7.2 0.6 collective-permute-start
  7.9 1.4 %collective-permute-done.2 = bf16[32,640]{1,0:T(8,128)(2,1)S(1)} collective-permute-done((bf16[32,640]{1,0:T(8,128)(2,1)S(1)}, bf16[32,640]{1,0:T(8,128)(2,1)S(1)}, u32[]{:S(2)}, u32[]{:S(2)}) %collective-permute-start.2) | collective-permute-done | bytes 40992 | tf_op jit(solution)/shard_map/ppermute | solution.py:83
  9.2 2.9 %collective-permute-done.1 = bf16[32,640]{1,0:T(8,128)(2,1)S(1)} collective-permute-done((bf16[32,640]{1,0:T(8,128)(2,1)S(1)}, bf16[32,640]{1,0:T(8,128)(2,1)S(1)}, u32[]{:S(2)}, u32[]{:S(2)}) %collective-permute-start.1) | collective-permute-done | bytes 40992 | tf_op jit(solution)/shard_map/ppermute | solution.py:83
  12.1 0.0 collective-permute-done
  12.1 0.8 %pad_maximum_fusion = bf16[128,640]{1,0:T(8,128)(2,1)S(1)} fusion(bf16[32,640]{1,0:T(8,128)(2,1)S(1)} %collective-permute-done.2, bf16[32,640]{1,0:T(8,128)(2,1)S(1)} %collective-permute-done.1, bf16[32,640]{1,0:T(8,128)(2,1)S(1)} %collective-permute-done, bf16[32,64]{1,0:T(8,128)(2,1)S(1)} %get-tuple-element.22, bf16[32,64]{1,0:T(8,128)(2,1)S(1)} %get-tuple-element.21, ...), kind=kLoop, calls=%fused_computation.22 | loop fusion | flops 983040 | bytes 327680 | tf_op jit(solution)/shard_map/concatenate | solution.py:93
  13.0 2.5 %collective-permute-start.5 = (bf16[128,640]{1,0:T(8,128)(2,1)S(1)}, bf16[128,640]{1,0:T(8,128)(2,1)S(1)}, u32[]{:S(2)}, u32[]{:S(2)}) collective-permute-start(bf16[128,640]{1,0:T(8,128)(2,1)S(1)} %pad_maximum_fusion), channel_id=1, source_target_pairs={{0,18},{1,19},{2,16},{3,17},{4,22},{5,23},{6,20},{7,21},{8,26},{9,... | collective-permute-start | bytes 491528 | tf_op jit(solution)/shard_map/ppermute | solution.py:83
  15.4 0.5 collective-permute-start.4
  15.9 0.5 collective-permute-start.3
  16.5 5.4 %collective-permute-done.3 = bf16[128,640]{1,0:T(8,128)(2,1)S(1)} collective-permute-done((bf16[128,640]{1,0:T(8,128)(2,1)S(1)}, bf16[128,640]{1,0:T(8,128)(2,1)S(1)}, u32[]{:S(2)}, u32[]{:S(2)}) %collective-permute-start.3) | collective-permute-done | bytes 163872 | tf_op jit(solution)/shard_map/ppermute | solution.py:83
  22.0 0.0 collective-permute-done.4
  22.1 0.0 collective-permute-done.5
  22.1 0.1 collective-permute-start.6
  22.2 2.1 %collective-permute-done.6 = bf16[512,640]{1,0:T(8,128)(2,1)S(1)} collective-permute-done((bf16[512,640]{1,0:T(8,128)(2,1)S(1)}, bf16[512,640]{1,0:T(8,128)(2,1)S(1)}, u32[]{:S(2)}, u32[]{:S(2)}) %collective-permute-start.6) | collective-permute-done | bytes 655392 | tf_op jit(solution)/shard_map/ppermute | solution.py:83
  24.3 0.1 constant_dynamic-update-slice_fusion.7
  24.4 0.3 multiply_reduce_fusion
  24.7 4.4 %fusion.24 = (f32[]{:T(128)}, f32[1024]{0:T(1024)S(1)}, f32[1024,1024]{0,1:T(8,128)}) fusion(bf16[1024,640]{1,0:T(8,128)(2,1)S(1)} %constant_dynamic-update-slice_fusion.7, f32[1024]{0:T(1024)S(1)} %multiply_reduce_fusion), kind=kOutput, calls=%fused_computation.61 | convolution fusion | flops 1083177984 | bytes 5255172 | tf_op jit(solution)/shard_map/dot_general | solution.py:114
  29.8 5.7 %fusion.1 = f32[1024,64]{0,1:T(8,128)S(1)} fusion(f32[1024,1024]{0,1:T(8,128)} %get-tuple-element.25, f32[1024]{0:T(1024)S(1)} %get-tuple-element.24, f32[1024]{0:T(1024)S(1)} %get-tuple-element.23, bf16[1024,640]{1,0:T(8,128)(2,1)S(1)} %constant_dynamic-update-slice_fusion.7), kind=kOutput, calls=%fused_computation.4 | convolution fusion | flops 809697280 | bytes 4997120 | tf_op jit(solution)/shard_map/dot_general | solution.py:128
  35.5 0.4 fusion.26
  35.9 0.1 copy.4
  36.0 5.8 %cholesky.44 = f32[64,64]{1,0:T(8,128)S(1)} custom-call(f32[64,64]{1,0:T(8,128)S(1)} %fusion.21), custom_call_target="Cholesky" | custom-call | tf_op jit(solution)/shard_map/jit(cholesky)/cholesky | solution.py:130
  41.9 0.6 compare_reduce_fusion.1
  42.5 0.7 fusion.16
  43.2 4.9 %custom-call.10 = f32[1,64,64]{1,2,0:T(8,128)S(1)} custom-call(f32[1,64,64]{2,1,0:T(8,128)S(1)} %fusion.16), custom_call_target="InvertDiagBlocksLowerTriangular" | custom-call | tf_op jit(solution)/shard_map/jit(_solve_triangular)/triangular_solve | solution.py:133
  48.1 1.0 %convolution_multiply_fusion = f32[1024,64]{1,0:T(8,128)S(1)} fusion(f32[1024,64]{0,1:T(8,128)S(1)} %fusion.1, f32[1,64,64]{1,2,0:T(8,128)S(1)} %custom-call.10), kind=kOutput, calls=%fused_computation.14 | convolution fusion | flops 50397184 | bytes 540672 | tf_op jit(solution)/shard_map/jit(_solve_triangular)/triangular_solve | solution.py:133
  49.1 5.7 %fusion = f32[1024,64]{0,1:T(8,128)S(1)} fusion(f32[1024,64]{1,0:T(8,128)S(1)} %convolution_multiply_fusion, f32[1024,1024]{0,1:T(8,128)} %get-tuple-element.25, f32[1024]{0:T(1024)S(1)} %get-tuple-element.24, f32[1024]{0:T(1024)S(1)} %get-tuple-element.23), kind=kOutput, calls=%fused_computation.3 | convolution fusion | flops 809500672 | bytes 4726784 | tf_op jit(solution)/shard_map/dot_general | solution.py:128
  54.9 0.4 fusion.27
  55.2 0.1 copy.5
  55.3 5.8 %cholesky.55 = f32[64,64]{1,0:T(8,128)S(1)} custom-call(f32[64,64]{1,0:T(8,128)S(1)} %fusion.19), custom_call_target="Cholesky" | custom-call | tf_op jit(solution)/shard_map/jit(cholesky)/cholesky | solution.py:130
  61.2 0.6 compare_reduce_fusion
  61.8 1.3 %select_bitcast_fusion = (f32[1,64,64]{2,1,0:T(8,128)S(1)}, f32[64,64]{1,0:T(8,128)}) fusion(f32[64,64]{1,0:T(8,128)S(1)} %cholesky.55, pred[]{:T(512)} %compare_reduce_fusion), kind=kLoop, calls=%fused_computation.52 | loop fusion | flops 16384 | bytes 49153 | tf_op jit(solution)/shard_map/jit(_solve_triangular)/triangular_solve | solution.py:133
  63.1 4.9 %custom-call.11 = f32[1,64,64]{1,2,0:T(8,128)S(1)} custom-call(f32[1,64,64]{2,1,0:T(8,128)S(1)} %get-tuple-element.5), custom_call_target="InvertDiagBlocksLowerTriangular" | custom-call | tf_op jit(solution)/shard_map/jit(_solve_triangular)/triangular_solve | solution.py:133
  68.0 0.8 %convolution_multiply_fusion.1 = f32[32,64]{1,0:T(8,128)} fusion(f32[1024,64]{0,1:T(8,128)S(1)} %fusion, f32[1,64,64]{1,2,0:T(8,128)S(1)} %custom-call.11), kind=kOutput, calls=%fused_computation.15 | convolution fusion | flops 1574912 | bytes 73728 | tf_op jit(solution)/shard_map/jit(_solve_triangular)/triangular_solve | solution.py:133
  (12 shorter events, 0.3 us)
Async XLA Ops:
  2.2 7.1 %collective-permute-start.2 = (bf16[32,640]{1,0:T(8,128)(2,1)S(1)}, bf16[32,640]{1,0:T(8,128)(2,1)S(1)}, u32[]{:S(2)}, u32[]{:S(2)}) collective-permute-start(bf16[32,640]{1,0:T(8,128)(2,1)S(1)} %get-tuple-element.8), channel_id=1, source_target_pairs={{0,12},{1,13},{2,14},{3,15},{4,8},{5,9},{6,10},{7,11},{8,4},{9,5},... | collective-permute-start | bytes 122888 | tf_op jit(solution)/shard_map/ppermute | solution.py:83
  7.2 4.9 %collective-permute-start.1 = (bf16[32,640]{1,0:T(8,128)(2,1)S(1)}, bf16[32,640]{1,0:T(8,128)(2,1)S(1)}, u32[]{:S(2)}, u32[]{:S(2)}) collective-permute-start(bf16[32,640]{1,0:T(8,128)(2,1)S(1)} %get-tuple-element.8), channel_id=1, source_target_pairs={{0,8},{1,9},{2,10},{3,11},{4,12},{5,13},{6,14},{7,15},{8,0},{9,1},... | collective-permute-start | bytes 122888 | tf_op jit(solution)/shard_map/ppermute | solution.py:83
  7.2 4.9 %collective-permute-start = (bf16[32,640]{1,0:T(8,128)(2,1)S(1)}, bf16[32,640]{1,0:T(8,128)(2,1)S(1)}, u32[]{:S(2)}, u32[]{:S(2)}) collective-permute-start(bf16[32,640]{1,0:T(8,128)(2,1)S(1)} %get-tuple-element.8), channel_id=1, source_target_pairs={{0,4},{1,5},{2,6},{3,7},{4,0},{5,1},{6,2},{7,3},{8,12},{9,13},{10,... | collective-permute-start | bytes 122888 | tf_op jit(solution)/shard_map/ppermute | solution.py:83
  13.0 9.1 %collective-permute-start.5 = (bf16[128,640]{1,0:T(8,128)(2,1)S(1)}, bf16[128,640]{1,0:T(8,128)(2,1)S(1)}, u32[]{:S(2)}, u32[]{:S(2)}) collective-permute-start(bf16[128,640]{1,0:T(8,128)(2,1)S(1)} %pad_maximum_fusion), channel_id=1, source_target_pairs={{0,18},{1,19},{2,16},{3,17},{4,22},{5,23},{6,20},{7,21},{8,26},{9,... | collective-permute-start | bytes 491528 | tf_op jit(solution)/shard_map/ppermute | solution.py:83
  15.4 6.6 %collective-permute-start.4 = (bf16[128,640]{1,0:T(8,128)(2,1)S(1)}, bf16[128,640]{1,0:T(8,128)(2,1)S(1)}, u32[]{:S(2)}, u32[]{:S(2)}) collective-permute-start(bf16[128,640]{1,0:T(8,128)(2,1)S(1)} %pad_maximum_fusion), channel_id=1, source_target_pairs={{0,16},{1,17},{2,18},{3,19},{4,20},{5,21},{6,22},{7,23},{8,24},{9,... | collective-permute-start | bytes 491528 | tf_op jit(solution)/shard_map/ppermute | solution.py:83
  15.9 6.0 %collective-permute-start.3 = (bf16[128,640]{1,0:T(8,128)(2,1)S(1)}, bf16[128,640]{1,0:T(8,128)(2,1)S(1)}, u32[]{:S(2)}, u32[]{:S(2)}) collective-permute-start(bf16[128,640]{1,0:T(8,128)(2,1)S(1)} %pad_maximum_fusion), channel_id=1, source_target_pairs={{0,2},{1,3},{2,0},{3,1},{4,6},{5,7},{6,4},{7,5},{8,10},{9,11},{10,... | collective-permute-start | bytes 491528 | tf_op jit(solution)/shard_map/ppermute | solution.py:83
  22.1 2.2 %collective-permute-start.6 = (bf16[512,640]{1,0:T(8,128)(2,1)S(1)}, bf16[512,640]{1,0:T(8,128)(2,1)S(1)}, u32[]{:S(2)}, u32[]{:S(2)}) collective-permute-start(bf16[512,640]{1,0:T(8,128)(2,1)S(1)} %get-tuple-element.9), channel_id=1, source_target_pairs={{0,1},{1,0},{2,3},{3,2},{4,5},{5,4},{6,7},{7,6},{8,9},{9,8},{10,11... | collective-permute-start | bytes 1966088 | tf_op jit(solution)/shard_map/ppermute | solution.py:83

commit v3 on v2

--- a/solution.py
+++ b/solution.py
@@ -1,13 +1,18 @@
+import functools
 import math
 
 import jax
 import jax.numpy as jnp
 from jax import lax
+from jax.experimental import pallas as pl
+from jax.experimental.pallas import tpu as pltpu
 from jax.sharding import PartitionSpec as P
 
 ITERS = 2
 AXES = ("row", "col", "vec")
 WHOLE_ROWS = 2048
+SAFE_PART = 1.0 / 16.0
+SAFE_SHARE = 1.0 / 8.0
 
 
 def sharded(particles, start_basis):
@@ -86,12 +91,231 @@
 def gather_all(block):
     sizes = tuple(lax.axis_size(name) for name in AXES)
     vec_size = sizes[2]
-    col_bits = [k * vec_size for k in range(1, sizes[1])]
     row_bit = sizes[1] * vec_size
-    plane_bits = [r * row_bit + v for r in range(sizes[0]) for v in range(0, vec_size, 2)][1:]
-    for bits in (col_bits, plane_bits, [1]):
-        block = jnp.concatenate([block] + [swap(block, sizes, k) for k in bits], axis=0)
-    return block
+    plane = [r * row_bit + v for r in range(sizes[0]) for v in range(0, vec_size, 2)][1:]
+    steps = sorted(range(1, sizes[1]), key=lambda k: (k != 2, -k))
+    line = {k: swap(block, sizes, k * vec_size) for k in steps}
+    sides = [swap(block, sizes, bits) for bits in plane]
+    along = jnp.concatenate([line[k] for k in steps], axis=0)
+    own = [jnp.concatenate([block] + sides, axis=0), along] + [swap(along, sizes, bits) for bits in plane]
+    return own + [swap(piece, sizes, 1) for piece in own]
+
+
+def split(value):
+    high = value.astype(jnp.bfloat16)
+    return high, (value - high.astype(jnp.float32)).astype(jnp.bfloat16)
+
+
+def mul(left, right, contract):
+    left_hi, left_lo = split(left)
+    right_hi, right_lo = right if isinstance(right, tuple) else split(right)
+    rows = left.shape[0]
+    dims = (((1,), (contract,)), ((), ()))
+    both = lax.dot_general(
+        jnp.concatenate([left_hi, left_lo], axis=0), right_hi, dims, preferred_element_type=jnp.float32
+    )
+    rest = lax.dot_general(left_hi, right_lo, dims, preferred_element_type=jnp.float32)
+    return both[:rows] + both[rows:] + rest
+
+
+def eliminate(grams):
+    size = grams[0].shape[0]
+    groups = size // 8
+    wide = 2 * size
+    eye = jnp.where(
+        lax.broadcasted_iota(jnp.int32, (size, size), 0) == lax.broadcasted_iota(jnp.int32, (size, size), 1),
+        jnp.float32(1.0),
+        jnp.float32(0.0),
+    )
+    sub = lax.broadcasted_iota(jnp.int32, (8, wide), 0)
+    works = []
+    for gram in grams:
+        work = jnp.concatenate([eye, gram], axis=1)
+        works.append([work[8 * g : 8 * g + 8] for g in range(groups)])
+    all_pivots = [[] for _ in grams]
+
+    def row(block, at):
+        return jnp.broadcast_to(block[at : at + 1], (8, wide))
+
+    def two_columns(cols, work, pivots, q, j):
+        first, both, second = row(cols[j][q], j), row(cols[j][q], j + 1), row(cols[j + 1][q], j + 1)
+        det = first * second - both * both
+        over_first = pl.reciprocal(first, approx=True)
+        over_second = pl.reciprocal(det, approx=True) * first
+        step = both * over_first
+        heads = {k: row(cols[k][q], j) for k in range(j + 2, 8)}
+        nexts = {k: row(cols[k][q], j + 1) - step * heads[k] for k in range(j + 2, 8)}
+        head_row = row(work[q], j)
+        next_row = row(work[q], j + 1) - step * head_row
+        for g in range(q, groups):
+            times = cols[j][g] * over_first
+            if g == q:
+                times = jnp.where(sub > j, times, 0.0)
+            again = (cols[j + 1][g] - times * both) * over_second
+            if g == q:
+                again = jnp.where(sub > j + 1, again, 0.0)
+            for k in range(j + 2, 8):
+                cols[k][g] = cols[k][g] - times * heads[k] - again * nexts[k]
+            work[g] = work[g] - times * head_row - again * next_row
+        pivots = jnp.where(sub == j, first, pivots)
+        return jnp.where(sub == j + 1, det * over_first, pivots)
+
+    for q in range(groups):
+        start = size + 8 * q
+        panels = [
+            [
+                {g: jnp.broadcast_to(work[g][:, start + j : start + j + 1], (8, wide)) for g in range(q, groups)}
+                for j in range(8)
+            ]
+            for work in works
+        ]
+        pivots = [panel[0][q] for panel in panels]
+        for j in range(0, 8, 2):
+            for m, work in enumerate(works):
+                pivots[m] = two_columns(panels[m], work, pivots[m], q, j)
+        for m, work in enumerate(works):
+            work[q] = work[q] * lax.rsqrt(pivots[m])
+            all_pivots[m].append(pivots[m])
+    return [
+        (jnp.concatenate(work, axis=0), jnp.concatenate(pivots, axis=0))
+        for work, pivots in zip(works, all_pivots)
+    ]
+
+
+def whole_kernel(width, eig_cols, *refs):
+    basis_ref, factor_ref, high_ref, low_ref, held_basis_ref, held_factor_ref, sems = refs[-7:]
+    total_rows = high_ref.shape[0]
+    tile = 128
+    count = total_rows // tile
+    packed = jnp.concatenate([piece[...] for piece in refs[:-7]], axis=0)
+    feats = packed[:, :width]
+    root_total = math.sqrt(float(total_rows))
+    spread = 2.0 * width
+    to_power = 2.0 / spread * math.log2(math.e)
+    tile_eye = lax.broadcasted_iota(jnp.int32, (tile, tile), 0) == lax.broadcasted_iota(
+        jnp.int32, (tile, tile), 1
+    )
+    weights = []
+    for i in range(count):
+        some = feats[i * tile : (i + 1) * tile].astype(jnp.float32)
+        weights.append(jnp.exp(jnp.sum(some * some, axis=1, keepdims=True) * (-1.0 / spread)))
+    def products(c):
+        columns = feats[c * tile : (c + 2) * tile]
+        return lax.dot_general(feats, columns, (((1,), (1,)), ((), ())), preferred_element_type=jnp.float32)
+
+    def fill(shift):
+        sums, squares = [], []
+        ahead = products(0)
+        for c in range(0, count, 2):
+            dots = ahead
+            if c + 2 < count:
+                ahead = products(c + 2)
+            for k in range(c, c + 2):
+                less = 1.0 if shift is None else shift[:, k * tile : (k + 1) * tile]
+                total = jnp.zeros((8, tile), jnp.float32)
+                for i in range(count):
+                    part = dots[i * tile : (i + 1) * tile, (k - c) * tile : (k - c + 1) * tile]
+                    grown = jnp.exp2(part * to_power)
+                    if i == k:
+                        squares.append(jnp.sum(jnp.where(tile_eye, part, 0.0), axis=0, keepdims=True))
+                        grown = jnp.where(tile_eye, 0.0, grown)
+                    total = total + jnp.sum((grown * weights[i]).reshape(tile // 8, 8, tile), axis=0)
+                    high, low = split(grown - less)
+                    high_ref[i * tile : (i + 1) * tile, k * tile : (k + 1) * tile] = high
+                    low_ref[i * tile : (i + 1) * tile, k * tile : (k + 1) * tile] = low
+                sums.append(jnp.sum(total, axis=0, keepdims=True))
+        return jnp.concatenate(sums, axis=1), jnp.concatenate(squares, axis=1)
+
+    sums, squares = fill(None)
+    weight = jnp.exp(squares * (-1.0 / spread))
+    degree = weight * sums
+    root_deg = jnp.sqrt(degree)
+    scale = weight / root_deg
+    root_vec = root_deg / jnp.sqrt(jnp.sum(degree, axis=1, keepdims=True))
+    turned = packed[:, width:].astype(jnp.float32).T
+    basis = turned[:eig_cols] + turned[eig_cols:]
+    basis = basis / jnp.max(jnp.abs(basis), axis=1, keepdims=True)
+    share = sums / jnp.sum(weight, axis=1, keepdims=True) - SAFE_SHARE
+
+    def deflate(vectors, shift=None):
+        scaled = vectors * scale
+        product = mul(scaled, (high_ref[...], low_ref[...]), 0)
+        whole_sum = jnp.sum(scaled, axis=1, keepdims=True)
+        product = product + (whole_sum if shift is None else whole_sum * shift)
+        return product * scale - jnp.sum(vectors * root_vec, axis=1, keepdims=True) * root_vec
+
+    rows_at = lax.broadcasted_iota(jnp.int32, (eig_cols, eig_cols), 0)
+    cols_at = lax.broadcasted_iota(jnp.int32, (eig_cols, eig_cols), 1)
+
+    copies = [
+        pltpu.make_async_copy(held_factor_ref, factor_ref, sems.at[0]),
+        pltpu.make_async_copy(held_basis_ref, basis_ref, sems.at[1]),
+    ]
+
+    def put(inverse, last, factor):
+        held_factor_ref[...] = jnp.where(rows_at >= cols_at, factor, 0.0)
+        copies[0].start()
+        held_basis_ref[...] = mul(inverse * root_total, last, 0).T[: basis_ref.shape[0]]
+        copies[1].start()
+
+    first = deflate(basis)
+    second = deflate(first)
+    grams = [mul(first, first, 1), mul(second, second, 1)]
+    (inner, inner_pivots), (outer, outer_pivots) = eliminate(grams)
+    put(
+        outer[:, :eig_cols],
+        second[:, :tile],
+        mul(inner[:, :eig_cols] * root_total, outer[:, eig_cols:], 1),
+    )
+    lengths = [
+        jnp.sum(jnp.where(rows_at == cols_at, gram, 0.0), axis=1, keepdims=True) for gram in grams
+    ]
+    safe = jnp.minimum(
+        jnp.min(inner_pivots - lengths[0] * SAFE_PART), jnp.min(outer_pivots - lengths[1] * SAFE_PART)
+    )
+    safe = jnp.minimum(safe, jnp.min(share))
+    for copy in copies:
+        copy.wait()
+
+    @pl.when(jnp.logical_not(safe > 0.0))
+    def one_sweep_after_the_other():
+        shift = jnp.where(share > 0.0, 1.0, 0.0)
+        fill(shift)
+        now = deflate(basis, shift)
+        ((solved, _),) = eliminate([mul(now, now, 1)])
+        now = mul(solved[:, :eig_cols] * root_total, now, 0)
+        now = deflate(now, shift)
+        ((solved, _),) = eliminate([mul(now, now, 1)])
+        put(solved[:, :eig_cols], now[:, :tile], solved[:, eig_cols:].T)
+        for copy in copies:
+            copy.wait()
+
+
+def whole(pieces, shard_rows, width, eig_cols):
+    total_rows = sum(piece.shape[0] for piece in pieces)
+    return pl.pallas_call(
+        functools.partial(whole_kernel, width, eig_cols),
+        out_shape=(
+            jax.ShapeDtypeStruct((shard_rows, eig_cols), jnp.float32),
+            jax.ShapeDtypeStruct((eig_cols, eig_cols), jnp.float32),
+        ),
+        in_specs=[pl.BlockSpec(memory_space=pltpu.VMEM)] * len(pieces),
+        out_specs=(pl.BlockSpec(memory_space=pltpu.HBM),) * 2,
+        scratch_shapes=[
+            pltpu.VMEM((total_rows, total_rows), jnp.bfloat16),
+            pltpu.VMEM((total_rows, total_rows), jnp.bfloat16),
+            pltpu.VMEM((shard_rows, eig_cols), jnp.float32),
+            pltpu.VMEM((eig_cols, eig_cols), jnp.float32),
+            pltpu.SemaphoreType.DMA((2,)),
+        ],
+        compiler_params=pltpu.CompilerParams(vmem_limit_bytes=40 * 1024 * 1024),
+        cost_estimate=pl.CostEstimate(
+            flops=2 * total_rows * total_rows * (width + 6 * eig_cols),
+            bytes_accessed=2 * total_rows * (width + 2 * eig_cols),
+            transcendentals=total_rows * total_rows,
+        ),
+        name="subspace_sweeps",
+    )(*pieces)
 
 
 def replicated(particles, start_basis):
@@ -102,36 +326,7 @@
     packed = jnp.concatenate(
         [particles, base_hi.astype(jnp.bfloat16), base_lo.astype(jnp.bfloat16)], axis=1
     )
-    everything = gather_all(packed)
-    feats = everything[:, :width]
-    basis = everything[:, width : width + eig_cols].astype(jnp.float32) + everything[
-        :, width + eig_cols : width + 2 * eig_cols
-    ].astype(jnp.float32)
-    total_rows = feats.shape[0]
-    spread = 2.0 * width
-    root_total = math.sqrt(float(total_rows))
-    squares = jnp.sum(jnp.square(feats.astype(jnp.float32)), axis=1)
-    inner_dots = lax.dot_general(
-        feats, feats, (((1,), (1,)), ((), ())), preferred_element_type=jnp.float32
-    )
-    distance = squares[:, None] + squares[None, :] - 2.0 * inner_dots
-    ids = jnp.arange(total_rows, dtype=jnp.int32)
-    kernel = jnp.where(ids[:, None] == ids[None, :], jnp.float32(0.0), jnp.exp(-distance / spread))
-    degree = jnp.sum(kernel, axis=1)
-    root_deg = jnp.sqrt(degree)
-    inv_root = 1.0 / root_deg
-    root_vec = root_deg / jnp.sqrt(jnp.sum(degree))
-    matrix = kernel * inv_root[:, None] * inv_root[None, :] - root_vec[:, None] * root_vec[None, :]
-    now = basis
-    factor = None
-    for sweep in range(ITERS):
-        now = jnp.dot(matrix, now, precision=lax.Precision.HIGHEST)
-        gram = jnp.dot(now.T, now, precision=lax.Precision.HIGHEST)
-        factor = jnp.linalg.cholesky(gram)
-        if sweep == ITERS - 1:
-            now = now[:shard_rows]
-        now = jax.scipy.linalg.solve_triangular(factor, now.T, lower=True).T * root_total
-    return (now, factor)
+    return whole(gather_all(packed), shard_rows, width, eig_cols)
 
 
 def local(particles, start_basis):

time: 69.3 us -> 35.7 us (0.52)
  other arithmetic: 27.4 us -> 0.89 us
  matrix products: 18.5 us -> 0 us
  Pallas kernels: 0 us -> 14.7 us
  waiting for transfers between devices: 11.8 us -> 5.5 us
  starting transfers between devices: 9.26 us -> 13.7 us
  between operations: 1.47 us -> 0.67 us
    another operation x10 -> x0, other arithmetic: 24.7 us -> none  [the longest x6 13 us: replicated(): factor = jnp.linalg.cholesky(gram)]
    dot_general x5 -> x0, matrix products: 16.6 us -> none  [the longest x2 11.4 us: replicated(): now = jnp.dot(matrix, now, precision=lax.Precision.HIGHEST)]
    pallas_call x0 -> x1, Pallas kernels: none -> 14.7 us  [whole(): pl.pallas_call(functools.partial(whole_kernel, width, eig_cols), out_shap...]
    ppermute x7 -> x14, waiting for transfers between devices: 11.8 us -> 5.5 us  [swap(): lax.ppermute(block, AXES, [(place, place ^ bits) for place in range(count)])]
    ppermute x7 -> x14, starting transfers between devices: 9.26 us -> 13.7 us  [swap(): lax.ppermute(block, AXES, [(place, place ^ bits) for place in range(count)])]
    another operation x2 -> x0, matrix products: 1.87 us -> none  [replicated(): jax.scipy.linalg.solve_triangular(factor, now.T, lower=True).T * root_total]
    unnamed x1 -> x0, other arithmetic: 0.84 us -> none
  transfers between devices with their start and end apart: 7 -> 14, of which waited for: 4 -> 6; matrix products, arithmetic and copies ran while one was open for 0% -> 0% of each run, Pallas kernels for 0% -> 0%
where the time goes in v3:
time: 35.7 us; the launch traced here: 35.5 us
  Pallas kernels  14.7 us (41%)
  starting transfers between devices  13.7 us (38%)
  waiting for transfers between devices  5.5 us (15%)
  other arithmetic  0.89 us (2%)
  between operations  0.67 us (2%)
    pallas_call x1, Pallas kernels, whole(): pl.pallas_call(functools.partial(whole_kernel, width, eig_cols), out_shap...  14.7 us
    ppermute x14, starting transfers between devices, swap(): lax.ppermute(block, AXES, [(place, place ^ bits) for place in range(count)])  13.7 us
    ppermute x14, waiting for transfers between devices, swap(): lax.ppermute(block, AXES, [(place, place ^ bits) for place in range(count)])  5.5 us
    convert_element_type x1, other arithmetic, replicated(): base_hi.astype(jnp.bfloat16)  0.73 us
  transfers between devices with their start and end apart: 14, of which 6 were waited for; matrix products, arithmetic and copies ran while one was open for 0% of the time, Pallas kernels for 0%

profile of v3, /device:TPU:0, one launch (start us, length us, event | category | flops | bytes accessed | tf_op | source)
XLA Modules:
  0.0 35.5 jit_solution(4742921442176418612)
XLA Ops:
  0.6 0.0 copy-start
  0.6 0.7 %reduce-precision_convert_fusion = (bf16[32,64]{1,0:T(8,128)(2,1)S(1)}, bf16[32,64]{1,0:T(8,128)(2,1)S(1)}) fusion(f32[32,64]{1,0:T(8,128)} %param.3), kind=kLoop, calls=%fused_computation.3 | loop fusion | flops 10240 | bytes 16384 | tf_op jit(solution)/shard_map/convert_element_type | solution.py:327
  1.4 0.0 copy-done
  1.4 0.1 pad_maximum_fusion.1
  1.5 4.0 %collective-permute-start.3 = (bf16[32,640]{1,0:T(8,128)(2,1)S(1)}, bf16[32,640]{1,0:T(8,128)(2,1)S(1)}, u32[]{:S(2)}, u32[]{:S(2)}) collective-permute-start(bf16[32,640]{1,0:T(8,128)(2,1)S(1)} %pad_maximum_fusion.1), channel_id=1, source_target_pairs={{0,8},{1,9},{2,10},{3,11},{4,12},{5,13},{6,14},{7,15},{8,0},{9,1},... | collective-permute-start | bytes 122888 | tf_op jit(solution)/shard_map/ppermute | solution.py:88
  5.5 1.3 %collective-permute-start.4 = (bf16[32,640]{1,0:T(8,128)(2,1)S(1)}, bf16[32,640]{1,0:T(8,128)(2,1)S(1)}, u32[]{:S(2)}, u32[]{:S(2)}) collective-permute-start(bf16[32,640]{1,0:T(8,128)(2,1)S(1)} %pad_maximum_fusion.1), channel_id=1, source_target_pairs={{0,12},{1,13},{2,14},{3,15},{4,8},{5,9},{6,10},{7,11},{8,4},{9,5},... | collective-permute-start | bytes 122888 | tf_op jit(solution)/shard_map/ppermute | solution.py:88
  6.9 0.2 collective-permute-start.5
  7.1 2.4 %collective-permute-start.2 = (bf16[32,640]{1,0:T(8,128)(2,1)S(1)}, bf16[32,640]{1,0:T(8,128)(2,1)S(1)}, u32[]{:S(2)}, u32[]{:S(2)}) collective-permute-start(bf16[32,640]{1,0:T(8,128)(2,1)S(1)} %pad_maximum_fusion.1), channel_id=1, source_target_pairs={{0,18},{1,19},{2,16},{3,17},{4,22},{5,23},{6,20},{7,21},{8,26},{9,... | collective-permute-start | bytes 122888 | tf_op jit(solution)/shard_map/ppermute | solution.py:88
  9.5 0.5 %collective-permute-start.1 = (bf16[32,640]{1,0:T(8,128)(2,1)S(1)}, bf16[32,640]{1,0:T(8,128)(2,1)S(1)}, u32[]{:S(2)}, u32[]{:S(2)}) collective-permute-start(bf16[32,640]{1,0:T(8,128)(2,1)S(1)} %pad_maximum_fusion.1), channel_id=1, source_target_pairs={{0,16},{1,17},{2,18},{3,19},{4,20},{5,21},{6,22},{7,23},{8,24},{9,... | collective-permute-start | bytes 122888 | tf_op jit(solution)/shard_map/ppermute | solution.py:88
  10.0 0.0 collective-permute-done.3
  10.0 0.5 %collective-permute-start = (bf16[32,640]{1,0:T(8,128)(2,1)S(1)}, bf16[32,640]{1,0:T(8,128)(2,1)S(1)}, u32[]{:S(2)}, u32[]{:S(2)}) collective-permute-start(bf16[32,640]{1,0:T(8,128)(2,1)S(1)} %pad_maximum_fusion.1), channel_id=1, source_target_pairs={{0,2},{1,3},{2,0},{3,1},{4,6},{5,7},{6,4},{7,5},{8,10},{9,11},{10,... | collective-permute-start | bytes 122888 | tf_op jit(solution)/shard_map/ppermute | solution.py:88
  10.6 0.7 %collective-permute-done.4 = bf16[32,640]{1,0:T(8,128)(2,1)S(1)} collective-permute-done((bf16[32,640]{1,0:T(8,128)(2,1)S(1)}, bf16[32,640]{1,0:T(8,128)(2,1)S(1)}, u32[]{:S(2)}, u32[]{:S(2)}) %collective-permute-start.4) | collective-permute-done | bytes 40992 | tf_op jit(solution)/shard_map/ppermute | solution.py:88
  11.3 0.0 collective-permute-done.5
  11.3 2.5 %collective-permute-start.8 = (bf16[96,640]{1,0:T(8,128)(2,1)S(1)}, bf16[96,640]{1,0:T(8,128)(2,1)S(1)}, u32[]{:S(2)}, u32[]{:S(2)}) collective-permute-start(bf16[96,640]{1,0:T(8,128)(2,1)S(1)} %constant_dynamic-update-slice_fusion.refs_1_), channel_id=1, source_target_pairs={{0,18},{1,19},{2,16},{3,17},{4,22},{5,23},{6,20},{7,21},{8,26},{9,... | collective-permute-start | bytes 368648 | tf_op jit(solution)/shard_map/ppermute | solution.py:88
  13.8 0.5 %collective-permute-start.7 = (bf16[96,640]{1,0:T(8,128)(2,1)S(1)}, bf16[96,640]{1,0:T(8,128)(2,1)S(1)}, u32[]{:S(2)}, u32[]{:S(2)}) collective-permute-start(bf16[96,640]{1,0:T(8,128)(2,1)S(1)} %constant_dynamic-update-slice_fusion.refs_1_), channel_id=1, source_target_pairs={{0,16},{1,17},{2,18},{3,19},{4,20},{5,21},{6,22},{7,23},{8,24},{9,... | collective-permute-start | bytes 368648 | tf_op jit(solution)/shard_map/ppermute | solution.py:88
  14.4 0.0 collective-permute-done.2
  14.4 0.5 %collective-permute-start.6 = (bf16[96,640]{1,0:T(8,128)(2,1)S(1)}, bf16[96,640]{1,0:T(8,128)(2,1)S(1)}, u32[]{:S(2)}, u32[]{:S(2)}) collective-permute-start(bf16[96,640]{1,0:T(8,128)(2,1)S(1)} %constant_dynamic-update-slice_fusion.refs_1_), channel_id=1, source_target_pairs={{0,2},{1,3},{2,0},{3,1},{4,6},{5,7},{6,4},{7,5},{8,10},{9,11},{10,... | collective-permute-start | bytes 368648 | tf_op jit(solution)/shard_map/ppermute | solution.py:88
  14.9 0.1 collective-permute-done.1
  15.0 0.0 collective-permute-done
  15.0 0.1 pad_maximum_fusion.refs_0_
  15.1 0.0 collective-permute-start.9
  15.1 0.5 %collective-permute-start.10 = (bf16[96,640]{1,0:T(8,128)(2,1)S(1)}, bf16[96,640]{1,0:T(8,128)(2,1)S(1)}, u32[]{:S(2)}, u32[]{:S(2)}) collective-permute-start(bf16[96,640]{1,0:T(8,128)(2,1)S(1)} %constant_dynamic-update-slice_fusion.refs_1_), channel_id=1, source_target_pairs={{0,1},{1,0},{2,3},{3,2},{4,5},{5,4},{6,7},{7,6},{8,9},{9,8},{10,11... | collective-permute-start | bytes 368648 | tf_op jit(solution)/shard_map/ppermute | solution.py:88
  15.6 2.9 %collective-permute-done.8.refs_4_ = bf16[96,640]{1,0:T(8,128)(2,1)S(1)} collective-permute-done((bf16[96,640]{1,0:T(8,128)(2,1)S(1)}, bf16[96,640]{1,0:T(8,128)(2,1)S(1)}, u32[]{:S(2)}, u32[]{:S(2)}) %collective-permute-start.8) | collective-permute-done | bytes 122912 | tf_op jit(solution)/shard_map/ppermute | solution.py:88
  18.5 0.0 collective-permute-start.13
  18.5 0.8 %collective-permute-done.7.refs_3_ = bf16[96,640]{1,0:T(8,128)(2,1)S(1)} collective-permute-done((bf16[96,640]{1,0:T(8,128)(2,1)S(1)}, bf16[96,640]{1,0:T(8,128)(2,1)S(1)}, u32[]{:S(2)}, u32[]{:S(2)}) %collective-permute-start.7) | collective-permute-done | bytes 122912 | tf_op jit(solution)/shard_map/ppermute | solution.py:88
  19.3 0.0 collective-permute-start.12
  19.3 0.0 collective-permute-done.6.refs_2_
  19.3 0.5 %collective-permute-start.11 = (bf16[96,640]{1,0:T(8,128)(2,1)S(1)}, bf16[96,640]{1,0:T(8,128)(2,1)S(1)}, u32[]{:S(2)}, u32[]{:S(2)}) collective-permute-start(bf16[96,640]{1,0:T(8,128)(2,1)S(1)} %collective-permute-done.6.refs_2_), channel_id=1, source_target_pairs={{0,1},{1,0},{2,3},{3,2},{4,5},{5,4},{6,7},{7,6},{8,9},{9,8},{10,11... | collective-permute-start | bytes 368648 | tf_op jit(solution)/shard_map/ppermute | solution.py:88
  19.8 0.0 collective-permute-done.10.refs_6_
  19.8 0.0 collective-permute-done.9.refs_5_
  19.8 0.0 collective-permute-done.13.refs_9_
  19.8 0.8 %collective-permute-done.12.refs_8_ = bf16[96,640]{1,0:T(8,128)(2,1)S(1)} collective-permute-done((bf16[96,640]{1,0:T(8,128)(2,1)S(1)}, bf16[96,640]{1,0:T(8,128)(2,1)S(1)}, u32[]{:S(2)}, u32[]{:S(2)}) %collective-permute-start.12) | collective-permute-done | bytes 122912 | tf_op jit(solution)/shard_map/ppermute | solution.py:88
  20.6 0.2 collective-permute-done.11.refs_7_
  20.8 14.7 %subspace_sweeps.1 = (f32[32,64]{1,0:T(8,128)}, f32[64,64]{1,0:T(8,128)}) custom-call(bf16[128,640]{1,0:T(8,128)(2,1)S(1)} %pad_maximum_fusion.refs_0_, bf16[96,640]{1,0:T(8,128)(2,1)S(1)} %constant_dynamic-update-slice_fusion.refs_1_, bf16[96,640]{1,0:T(8,128)(2,1)S(1)} %collective-permute-done.6.refs_2_, ...), custom_call_target="tpu_custom_call" | custom-call | flops 1879048192 | bytes 1310720 | tf_op jit(solution)/shard_map/subspace_sweeps/pallas_call | solution.py:296
  (3 shorter events, 0.0 us)
Async XLA Ops:
  0.6 0.8 %copy-start = (bf16[32,512]{1,0:T(8,128)(2,1)S(1)}, bf16[32,512]{1,0:T(8,128)(2,1)}, u32[]{:S(2)}) copy-start(bf16[32,512]{1,0:T(8,128)(2,1)} %param.2) | copy-start | bytes 98308
  1.5 8.6 %collective-permute-start.3 = (bf16[32,640]{1,0:T(8,128)(2,1)S(1)}, bf16[32,640]{1,0:T(8,128)(2,1)S(1)}, u32[]{:S(2)}, u32[]{:S(2)}) collective-permute-start(bf16[32,640]{1,0:T(8,128)(2,1)S(1)} %pad_maximum_fusion.1), channel_id=1, source_target_pairs={{0,8},{1,9},{2,10},{3,11},{4,12},{5,13},{6,14},{7,15},{8,0},{9,1},... | collective-permute-start | bytes 122888 | tf_op jit(solution)/shard_map/ppermute | solution.py:88
  5.5 5.8 %collective-permute-start.4 = (bf16[32,640]{1,0:T(8,128)(2,1)S(1)}, bf16[32,640]{1,0:T(8,128)(2,1)S(1)}, u32[]{:S(2)}, u32[]{:S(2)}) collective-permute-start(bf16[32,640]{1,0:T(8,128)(2,1)S(1)} %pad_maximum_fusion.1), channel_id=1, source_target_pairs={{0,12},{1,13},{2,14},{3,15},{4,8},{5,9},{6,10},{7,11},{8,4},{9,5},... | collective-permute-start | bytes 122888 | tf_op jit(solution)/shard_map/ppermute | solution.py:88
  6.9 4.5 %collective-permute-start.5 = (bf16[32,640]{1,0:T(8,128)(2,1)S(1)}, bf16[32,640]{1,0:T(8,128)(2,1)S(1)}, u32[]{:S(2)}, u32[]{:S(2)}) collective-permute-start(bf16[32,640]{1,0:T(8,128)(2,1)S(1)} %pad_maximum_fusion.1), channel_id=1, source_target_pairs={{0,4},{1,5},{2,6},{3,7},{4,0},{5,1},{6,2},{7,3},{8,12},{9,13},{10,... | collective-permute-start | bytes 122888 | tf_op jit(solution)/shard_map/ppermute | solution.py:88
  7.1 7.3 %collective-permute-start.2 = (bf16[32,640]{1,0:T(8,128)(2,1)S(1)}, bf16[32,640]{1,0:T(8,128)(2,1)S(1)}, u32[]{:S(2)}, u32[]{:S(2)}) collective-permute-start(bf16[32,640]{1,0:T(8,128)(2,1)S(1)} %pad_maximum_fusion.1), channel_id=1, source_target_pairs={{0,18},{1,19},{2,16},{3,17},{4,22},{5,23},{6,20},{7,21},{8,26},{9,... | collective-permute-start | bytes 122888 | tf_op jit(solution)/shard_map/ppermute | solution.py:88
  9.5 5.5 %collective-permute-start.1 = (bf16[32,640]{1,0:T(8,128)(2,1)S(1)}, bf16[32,640]{1,0:T(8,128)(2,1)S(1)}, u32[]{:S(2)}, u32[]{:S(2)}) collective-permute-start(bf16[32,640]{1,0:T(8,128)(2,1)S(1)} %pad_maximum_fusion.1), channel_id=1, source_target_pairs={{0,16},{1,17},{2,18},{3,19},{4,20},{5,21},{6,22},{7,23},{8,24},{9,... | collective-permute-start | bytes 122888 | tf_op jit(solution)/shard_map/ppermute | solution.py:88
  10.0 4.9 %collective-permute-start = (bf16[32,640]{1,0:T(8,128)(2,1)S(1)}, bf16[32,640]{1,0:T(8,128)(2,1)S(1)}, u32[]{:S(2)}, u32[]{:S(2)}) collective-permute-start(bf16[32,640]{1,0:T(8,128)(2,1)S(1)} %pad_maximum_fusion.1), channel_id=1, source_target_pairs={{0,2},{1,3},{2,0},{3,1},{4,6},{5,7},{6,4},{7,5},{8,10},{9,11},{10,... | collective-permute-start | bytes 122888 | tf_op jit(solution)/shard_map/ppermute | solution.py:88
  11.3 7.2 %collective-permute-start.8 = (bf16[96,640]{1,0:T(8,128)(2,1)S(1)}, bf16[96,640]{1,0:T(8,128)(2,1)S(1)}, u32[]{:S(2)}, u32[]{:S(2)}) collective-permute-start(bf16[96,640]{1,0:T(8,128)(2,1)S(1)} %constant_dynamic-update-slice_fusion.refs_1_), channel_id=1, source_target_pairs={{0,18},{1,19},{2,16},{3,17},{4,22},{5,23},{6,20},{7,21},{8,26},{9,... | collective-permute-start | bytes 368648 | tf_op jit(solution)/shard_map/ppermute | solution.py:88
  13.8 5.4 %collective-permute-start.7 = (bf16[96,640]{1,0:T(8,128)(2,1)S(1)}, bf16[96,640]{1,0:T(8,128)(2,1)S(1)}, u32[]{:S(2)}, u32[]{:S(2)}) collective-permute-start(bf16[96,640]{1,0:T(8,128)(2,1)S(1)} %constant_dynamic-update-slice_fusion.refs_1_), channel_id=1, source_target_pairs={{0,16},{1,17},{2,18},{3,19},{4,20},{5,21},{6,22},{7,23},{8,24},{9,... | collective-permute-start | bytes 368648 | tf_op jit(solution)/shard_map/ppermute | solution.py:88
  14.4 4.9 %collective-permute-start.6 = (bf16[96,640]{1,0:T(8,128)(2,1)S(1)}, bf16[96,640]{1,0:T(8,128)(2,1)S(1)}, u32[]{:S(2)}, u32[]{:S(2)}) collective-permute-start(bf16[96,640]{1,0:T(8,128)(2,1)S(1)} %constant_dynamic-update-slice_fusion.refs_1_), channel_id=1, source_target_pairs={{0,2},{1,3},{2,0},{3,1},{4,6},{5,7},{6,4},{7,5},{8,10},{9,11},{10,... | collective-permute-start | bytes 368648 | tf_op jit(solution)/shard_map/ppermute | solution.py:88
  15.1 4.7 %collective-permute-start.9 = (bf16[128,640]{1,0:T(8,128)(2,1)S(1)}, bf16[128,640]{1,0:T(8,128)(2,1)S(1)}, u32[]{:S(2)}, u32[]{:S(2)}) collective-permute-start(bf16[128,640]{1,0:T(8,128)(2,1)S(1)} %pad_maximum_fusion.refs_0_), channel_id=1, source_target_pairs={{0,1},{1,0},{2,3},{3,2},{4,5},{5,4},{6,7},{7,6},{8,9},{9,8},{10,11... | collective-permute-start | bytes 491528 | tf_op jit(solution)/shard_map/ppermute | solution.py:88
  15.1 4.7 %collective-permute-start.10 = (bf16[96,640]{1,0:T(8,128)(2,1)S(1)}, bf16[96,640]{1,0:T(8,128)(2,1)S(1)}, u32[]{:S(2)}, u32[]{:S(2)}) collective-permute-start(bf16[96,640]{1,0:T(8,128)(2,1)S(1)} %constant_dynamic-update-slice_fusion.refs_1_), channel_id=1, source_target_pairs={{0,1},{1,0},{2,3},{3,2},{4,5},{5,4},{6,7},{7,6},{8,9},{9,8},{10,11... | collective-permute-start | bytes 368648 | tf_op jit(solution)/shard_map/ppermute | solution.py:88
  18.5 1.3 %collective-permute-start.13 = (bf16[96,640]{1,0:T(8,128)(2,1)S(1)}, bf16[96,640]{1,0:T(8,128)(2,1)S(1)}, u32[]{:S(2)}, u32[]{:S(2)}) collective-permute-start(bf16[96,640]{1,0:T(8,128)(2,1)S(1)} %collective-permute-done.8.refs_4_), channel_id=1, source_target_pairs={{0,1},{1,0},{2,3},{3,2},{4,5},{5,4},{6,7},{7,6},{8,9},{9,8},{10,11... | collective-permute-start | bytes 368648 | tf_op jit(solution)/shard_map/ppermute | solution.py:88
  19.3 1.3 %collective-permute-start.12 = (bf16[96,640]{1,0:T(8,128)(2,1)S(1)}, bf16[96,640]{1,0:T(8,128)(2,1)S(1)}, u32[]{:S(2)}, u32[]{:S(2)}) collective-permute-start(bf16[96,640]{1,0:T(8,128)(2,1)S(1)} %collective-permute-done.7.refs_3_), channel_id=1, source_target_pairs={{0,1},{1,0},{2,3},{3,2},{4,5},{5,4},{6,7},{7,6},{8,9},{9,8},{10,11... | collective-permute-start | bytes 368648 | tf_op jit(solution)/shard_map/ppermute | solution.py:88
  19.3 1.5 %collective-permute-start.11 = (bf16[96,640]{1,0:T(8,128)(2,1)S(1)}, bf16[96,640]{1,0:T(8,128)(2,1)S(1)}, u32[]{:S(2)}, u32[]{:S(2)}) collective-permute-start(bf16[96,640]{1,0:T(8,128)(2,1)S(1)} %collective-permute-done.6.refs_2_), channel_id=1, source_target_pairs={{0,1},{1,0},{2,3},{3,2},{4,5},{5,4},{6,7},{7,6},{8,9},{9,8},{10,11... | collective-permute-start | bytes 368648 | tf_op jit(solution)/shard_map/ppermute | solution.py:88

commit v4 on v3

--- a/solution.py
+++ b/solution.py
@@ -183,11 +183,12 @@
 
 
 def whole_kernel(width, eig_cols, *refs):
-    basis_ref, factor_ref, high_ref, low_ref, held_basis_ref, held_factor_ref, sems = refs[-7:]
-    total_rows = high_ref.shape[0]
+    basis_ref, factor_ref, pair_ref, held_basis_ref, held_factor_ref, sems = refs[-6:]
+    total_rows = pair_ref.shape[1]
+    high_ref, low_ref = pair_ref.at[:total_rows], pair_ref.at[total_rows:]
     tile = 128
     count = total_rows // tile
-    packed = jnp.concatenate([piece[...] for piece in refs[:-7]], axis=0)
+    packed = jnp.concatenate([piece[...] for piece in refs[:-6]], axis=0)
     feats = packed[:, :width]
     root_total = math.sqrt(float(total_rows))
     spread = 2.0 * width
@@ -239,7 +240,11 @@
 
     def deflate(vectors, shift=None):
         scaled = vectors * scale
-        product = mul(scaled, (high_ref[...], low_ref[...]), 0)
+        parts = jnp.concatenate(split(scaled), axis=0)
+        product = jnp.dot(
+            jnp.concatenate([parts, parts], axis=1), pair_ref[...], preferred_element_type=jnp.float32
+        )
+        product = product[:eig_cols] + product[eig_cols:]
         whole_sum = jnp.sum(scaled, axis=1, keepdims=True)
         product = product + (whole_sum if shift is None else whole_sum * shift)
         return product * scale - jnp.sum(vectors * root_vec, axis=1, keepdims=True) * root_vec
@@ -302,8 +307,7 @@
         in_specs=[pl.BlockSpec(memory_space=pltpu.VMEM)] * len(pieces),
         out_specs=(pl.BlockSpec(memory_space=pltpu.HBM),) * 2,
         scratch_shapes=[
-            pltpu.VMEM((total_rows, total_rows), jnp.bfloat16),
-            pltpu.VMEM((total_rows, total_rows), jnp.bfloat16),
+            pltpu.VMEM((2 * total_rows, total_rows), jnp.bfloat16),
             pltpu.VMEM((shard_rows, eig_cols), jnp.float32),
             pltpu.VMEM((eig_cols, eig_cols), jnp.float32),
             pltpu.SemaphoreType.DMA((2,)),

time: 35.7 us -> 35.5 us (level)
  no operation moved by 1% of the time
where the time goes in v4:
time: 35.5 us; the launch traced here: 35.3 us
  Pallas kernels  14.5 us (41%)
  starting transfers between devices  13.7 us (39%)
  waiting for transfers between devices  5.5 us (15%)
  other arithmetic  0.89 us (3%)
  between operations  0.67 us (2%)
    pallas_call x1, Pallas kernels, whole(): pl.pallas_call(functools.partial(whole_kernel, width, eig_cols), out_shap...  14.5 us
    ppermute x14, starting transfers between devices, swap(): lax.ppermute(block, AXES, [(place, place ^ bits) for place in range(count)])  13.7 us
    ppermute x14, waiting for transfers between devices, swap(): lax.ppermute(block, AXES, [(place, place ^ bits) for place in range(count)])  5.5 us
    convert_element_type x1, other arithmetic, replicated(): base_hi.astype(jnp.bfloat16)  0.73 us
  transfers between devices with their start and end apart: 14, of which 6 were waited for; matrix products, arithmetic and copies ran while one was open for 0% of the time, Pallas kernels for 0%

profile of v4, /device:TPU:0, one launch (start us, length us, event | category | flops | bytes accessed | tf_op | source)
XLA Modules:
  0.0 35.3 jit_solution(5668255932784491758)
XLA Ops:
  0.6 0.0 copy-start
  0.6 0.7 %reduce-precision_convert_fusion = (bf16[32,64]{1,0:T(8,128)(2,1)S(1)}, bf16[32,64]{1,0:T(8,128)(2,1)S(1)}) fusion(f32[32,64]{1,0:T(8,128)} %param.3), kind=kLoop, calls=%fused_computation.3 | loop fusion | flops 10240 | bytes 16384 | tf_op jit(solution)/shard_map/convert_element_type | solution.py:331
  1.4 0.0 copy-done
  1.4 0.1 pad_maximum_fusion.1
  1.5 4.0 %collective-permute-start.3 = (bf16[32,640]{1,0:T(8,128)(2,1)S(1)}, bf16[32,640]{1,0:T(8,128)(2,1)S(1)}, u32[]{:S(2)}, u32[]{:S(2)}) collective-permute-start(bf16[32,640]{1,0:T(8,128)(2,1)S(1)} %pad_maximum_fusion.1), channel_id=1, source_target_pairs={{0,8},{1,9},{2,10},{3,11},{4,12},{5,13},{6,14},{7,15},{8,0},{9,1},... | collective-permute-start | bytes 122888 | tf_op jit(solution)/shard_map/ppermute | solution.py:88
  5.5 1.3 %collective-permute-start.4 = (bf16[32,640]{1,0:T(8,128)(2,1)S(1)}, bf16[32,640]{1,0:T(8,128)(2,1)S(1)}, u32[]{:S(2)}, u32[]{:S(2)}) collective-permute-start(bf16[32,640]{1,0:T(8,128)(2,1)S(1)} %pad_maximum_fusion.1), channel_id=1, source_target_pairs={{0,12},{1,13},{2,14},{3,15},{4,8},{5,9},{6,10},{7,11},{8,4},{9,5},... | collective-permute-start | bytes 122888 | tf_op jit(solution)/shard_map/ppermute | solution.py:88
  6.9 0.2 collective-permute-start.5
  7.1 2.4 %collective-permute-start.2 = (bf16[32,640]{1,0:T(8,128)(2,1)S(1)}, bf16[32,640]{1,0:T(8,128)(2,1)S(1)}, u32[]{:S(2)}, u32[]{:S(2)}) collective-permute-start(bf16[32,640]{1,0:T(8,128)(2,1)S(1)} %pad_maximum_fusion.1), channel_id=1, source_target_pairs={{0,18},{1,19},{2,16},{3,17},{4,22},{5,23},{6,20},{7,21},{8,26},{9,... | collective-permute-start | bytes 122888 | tf_op jit(solution)/shard_map/ppermute | solution.py:88
  9.5 0.5 %collective-permute-start.1 = (bf16[32,640]{1,0:T(8,128)(2,1)S(1)}, bf16[32,640]{1,0:T(8,128)(2,1)S(1)}, u32[]{:S(2)}, u32[]{:S(2)}) collective-permute-start(bf16[32,640]{1,0:T(8,128)(2,1)S(1)} %pad_maximum_fusion.1), channel_id=1, source_target_pairs={{0,16},{1,17},{2,18},{3,19},{4,20},{5,21},{6,22},{7,23},{8,24},{9,... | collective-permute-start | bytes 122888 | tf_op jit(solution)/shard_map/ppermute | solution.py:88
  10.0 0.0 collective-permute-done.3
  10.0 0.5 %collective-permute-start = (bf16[32,640]{1,0:T(8,128)(2,1)S(1)}, bf16[32,640]{1,0:T(8,128)(2,1)S(1)}, u32[]{:S(2)}, u32[]{:S(2)}) collective-permute-start(bf16[32,640]{1,0:T(8,128)(2,1)S(1)} %pad_maximum_fusion.1), channel_id=1, source_target_pairs={{0,2},{1,3},{2,0},{3,1},{4,6},{5,7},{6,4},{7,5},{8,10},{9,11},{10,... | collective-permute-start | bytes 122888 | tf_op jit(solution)/shard_map/ppermute | solution.py:88
  10.6 0.7 %collective-permute-done.4 = bf16[32,640]{1,0:T(8,128)(2,1)S(1)} collective-permute-done((bf16[32,640]{1,0:T(8,128)(2,1)S(1)}, bf16[32,640]{1,0:T(8,128)(2,1)S(1)}, u32[]{:S(2)}, u32[]{:S(2)}) %collective-permute-start.4) | collective-permute-done | bytes 40992 | tf_op jit(solution)/shard_map/ppermute | solution.py:88
  11.3 0.0 collective-permute-done.5
  11.3 2.5 %collective-permute-start.8 = (bf16[96,640]{1,0:T(8,128)(2,1)S(1)}, bf16[96,640]{1,0:T(8,128)(2,1)S(1)}, u32[]{:S(2)}, u32[]{:S(2)}) collective-permute-start(bf16[96,640]{1,0:T(8,128)(2,1)S(1)} %constant_dynamic-update-slice_fusion.refs_1_), channel_id=1, source_target_pairs={{0,18},{1,19},{2,16},{3,17},{4,22},{5,23},{6,20},{7,21},{8,26},{9,... | collective-permute-start | bytes 368648 | tf_op jit(solution)/shard_map/ppermute | solution.py:88
  13.8 0.5 %collective-permute-start.7 = (bf16[96,640]{1,0:T(8,128)(2,1)S(1)}, bf16[96,640]{1,0:T(8,128)(2,1)S(1)}, u32[]{:S(2)}, u32[]{:S(2)}) collective-permute-start(bf16[96,640]{1,0:T(8,128)(2,1)S(1)} %constant_dynamic-update-slice_fusion.refs_1_), channel_id=1, source_target_pairs={{0,16},{1,17},{2,18},{3,19},{4,20},{5,21},{6,22},{7,23},{8,24},{9,... | collective-permute-start | bytes 368648 | tf_op jit(solution)/shard_map/ppermute | solution.py:88
  14.4 0.0 collective-permute-done.2
  14.4 0.5 %collective-permute-start.6 = (bf16[96,640]{1,0:T(8,128)(2,1)S(1)}, bf16[96,640]{1,0:T(8,128)(2,1)S(1)}, u32[]{:S(2)}, u32[]{:S(2)}) collective-permute-start(bf16[96,640]{1,0:T(8,128)(2,1)S(1)} %constant_dynamic-update-slice_fusion.refs_1_), channel_id=1, source_target_pairs={{0,2},{1,3},{2,0},{3,1},{4,6},{5,7},{6,4},{7,5},{8,10},{9,11},{10,... | collective-permute-start | bytes 368648 | tf_op jit(solution)/shard_map/ppermute | solution.py:88
  14.9 0.1 collective-permute-done.1
  15.0 0.0 collective-permute-done
  15.0 0.1 pad_maximum_fusion.refs_0_
  15.1 0.0 collective-permute-start.9
  15.1 0.5 %collective-permute-start.10 = (bf16[96,640]{1,0:T(8,128)(2,1)S(1)}, bf16[96,640]{1,0:T(8,128)(2,1)S(1)}, u32[]{:S(2)}, u32[]{:S(2)}) collective-permute-start(bf16[96,640]{1,0:T(8,128)(2,1)S(1)} %constant_dynamic-update-slice_fusion.refs_1_), channel_id=1, source_target_pairs={{0,1},{1,0},{2,3},{3,2},{4,5},{5,4},{6,7},{7,6},{8,9},{9,8},{10,11... | collective-permute-start | bytes 368648 | tf_op jit(solution)/shard_map/ppermute | solution.py:88
  15.6 2.9 %collective-permute-done.8.refs_4_ = bf16[96,640]{1,0:T(8,128)(2,1)S(1)} collective-permute-done((bf16[96,640]{1,0:T(8,128)(2,1)S(1)}, bf16[96,640]{1,0:T(8,128)(2,1)S(1)}, u32[]{:S(2)}, u32[]{:S(2)}) %collective-permute-start.8) | collective-permute-done | bytes 122912 | tf_op jit(solution)/shard_map/ppermute | solution.py:88
  18.5 0.0 collective-permute-start.13
  18.5 0.8 %collective-permute-done.7.refs_3_ = bf16[96,640]{1,0:T(8,128)(2,1)S(1)} collective-permute-done((bf16[96,640]{1,0:T(8,128)(2,1)S(1)}, bf16[96,640]{1,0:T(8,128)(2,1)S(1)}, u32[]{:S(2)}, u32[]{:S(2)}) %collective-permute-start.7) | collective-permute-done | bytes 122912 | tf_op jit(solution)/shard_map/ppermute | solution.py:88
  19.3 0.0 collective-permute-start.12
  19.3 0.0 collective-permute-done.6.refs_2_
  19.3 0.5 %collective-permute-start.11 = (bf16[96,640]{1,0:T(8,128)(2,1)S(1)}, bf16[96,640]{1,0:T(8,128)(2,1)S(1)}, u32[]{:S(2)}, u32[]{:S(2)}) collective-permute-start(bf16[96,640]{1,0:T(8,128)(2,1)S(1)} %collective-permute-done.6.refs_2_), channel_id=1, source_target_pairs={{0,1},{1,0},{2,3},{3,2},{4,5},{5,4},{6,7},{7,6},{8,9},{9,8},{10,11... | collective-permute-start | bytes 368648 | tf_op jit(solution)/shard_map/ppermute | solution.py:88
  19.8 0.0 collective-permute-done.10.refs_6_
  19.8 0.0 collective-permute-done.9.refs_5_
  19.8 0.0 collective-permute-done.13.refs_9_
  19.8 0.8 %collective-permute-done.12.refs_8_ = bf16[96,640]{1,0:T(8,128)(2,1)S(1)} collective-permute-done((bf16[96,640]{1,0:T(8,128)(2,1)S(1)}, bf16[96,640]{1,0:T(8,128)(2,1)S(1)}, u32[]{:S(2)}, u32[]{:S(2)}) %collective-permute-start.12) | collective-permute-done | bytes 122912 | tf_op jit(solution)/shard_map/ppermute | solution.py:88
  20.6 0.2 collective-permute-done.11.refs_7_
  20.8 14.5 %subspace_sweeps.1 = (f32[32,64]{1,0:T(8,128)}, f32[64,64]{1,0:T(8,128)}) custom-call(bf16[128,640]{1,0:T(8,128)(2,1)S(1)} %pad_maximum_fusion.refs_0_, bf16[96,640]{1,0:T(8,128)(2,1)S(1)} %constant_dynamic-update-slice_fusion.refs_1_, bf16[96,640]{1,0:T(8,128)(2,1)S(1)} %collective-permute-done.6.refs_2_, ...), custom_call_target="tpu_custom_call" | custom-call | flops 1879048192 | bytes 1310720 | tf_op jit(solution)/shard_map/subspace_sweeps/pallas_call | solution.py:301
  (3 shorter events, 0.0 us)
Async XLA Ops:
  0.6 0.8 %copy-start = (bf16[32,512]{1,0:T(8,128)(2,1)S(1)}, bf16[32,512]{1,0:T(8,128)(2,1)}, u32[]{:S(2)}) copy-start(bf16[32,512]{1,0:T(8,128)(2,1)} %param.2) | copy-start | bytes 98308
  1.5 8.6 %collective-permute-start.3 = (bf16[32,640]{1,0:T(8,128)(2,1)S(1)}, bf16[32,640]{1,0:T(8,128)(2,1)S(1)}, u32[]{:S(2)}, u32[]{:S(2)}) collective-permute-start(bf16[32,640]{1,0:T(8,128)(2,1)S(1)} %pad_maximum_fusion.1), channel_id=1, source_target_pairs={{0,8},{1,9},{2,10},{3,11},{4,12},{5,13},{6,14},{7,15},{8,0},{9,1},... | collective-permute-start | bytes 122888 | tf_op jit(solution)/shard_map/ppermute | solution.py:88
  5.5 5.8 %collective-permute-start.4 = (bf16[32,640]{1,0:T(8,128)(2,1)S(1)}, bf16[32,640]{1,0:T(8,128)(2,1)S(1)}, u32[]{:S(2)}, u32[]{:S(2)}) collective-permute-start(bf16[32,640]{1,0:T(8,128)(2,1)S(1)} %pad_maximum_fusion.1), channel_id=1, source_target_pairs={{0,12},{1,13},{2,14},{3,15},{4,8},{5,9},{6,10},{7,11},{8,4},{9,5},... | collective-permute-start | bytes 122888 | tf_op jit(solution)/shard_map/ppermute | solution.py:88
  6.9 4.5 %collective-permute-start.5 = (bf16[32,640]{1,0:T(8,128)(2,1)S(1)}, bf16[32,640]{1,0:T(8,128)(2,1)S(1)}, u32[]{:S(2)}, u32[]{:S(2)}) collective-permute-start(bf16[32,640]{1,0:T(8,128)(2,1)S(1)} %pad_maximum_fusion.1), channel_id=1, source_target_pairs={{0,4},{1,5},{2,6},{3,7},{4,0},{5,1},{6,2},{7,3},{8,12},{9,13},{10,... | collective-permute-start | bytes 122888 | tf_op jit(solution)/shard_map/ppermute | solution.py:88
  7.1 7.3 %collective-permute-start.2 = (bf16[32,640]{1,0:T(8,128)(2,1)S(1)}, bf16[32,640]{1,0:T(8,128)(2,1)S(1)}, u32[]{:S(2)}, u32[]{:S(2)}) collective-permute-start(bf16[32,640]{1,0:T(8,128)(2,1)S(1)} %pad_maximum_fusion.1), channel_id=1, source_target_pairs={{0,18},{1,19},{2,16},{3,17},{4,22},{5,23},{6,20},{7,21},{8,26},{9,... | collective-permute-start | bytes 122888 | tf_op jit(solution)/shard_map/ppermute | solution.py:88
  9.5 5.5 %collective-permute-start.1 = (bf16[32,640]{1,0:T(8,128)(2,1)S(1)}, bf16[32,640]{1,0:T(8,128)(2,1)S(1)}, u32[]{:S(2)}, u32[]{:S(2)}) collective-permute-start(bf16[32,640]{1,0:T(8,128)(2,1)S(1)} %pad_maximum_fusion.1), channel_id=1, source_target_pairs={{0,16},{1,17},{2,18},{3,19},{4,20},{5,21},{6,22},{7,23},{8,24},{9,... | collective-permute-start | bytes 122888 | tf_op jit(solution)/shard_map/ppermute | solution.py:88
  10.0 4.9 %collective-permute-start = (bf16[32,640]{1,0:T(8,128)(2,1)S(1)}, bf16[32,640]{1,0:T(8,128)(2,1)S(1)}, u32[]{:S(2)}, u32[]{:S(2)}) collective-permute-start(bf16[32,640]{1,0:T(8,128)(2,1)S(1)} %pad_maximum_fusion.1), channel_id=1, source_target_pairs={{0,2},{1,3},{2,0},{3,1},{4,6},{5,7},{6,4},{7,5},{8,10},{9,11},{10,... | collective-permute-start | bytes 122888 | tf_op jit(solution)/shard_map/ppermute | solution.py:88
  11.3 7.2 %collective-permute-start.8 = (bf16[96,640]{1,0:T(8,128)(2,1)S(1)}, bf16[96,640]{1,0:T(8,128)(2,1)S(1)}, u32[]{:S(2)}, u32[]{:S(2)}) collective-permute-start(bf16[96,640]{1,0:T(8,128)(2,1)S(1)} %constant_dynamic-update-slice_fusion.refs_1_), channel_id=1, source_target_pairs={{0,18},{1,19},{2,16},{3,17},{4,22},{5,23},{6,20},{7,21},{8,26},{9,... | collective-permute-start | bytes 368648 | tf_op jit(solution)/shard_map/ppermute | solution.py:88
  13.8 5.4 %collective-permute-start.7 = (bf16[96,640]{1,0:T(8,128)(2,1)S(1)}, bf16[96,640]{1,0:T(8,128)(2,1)S(1)}, u32[]{:S(2)}, u32[]{:S(2)}) collective-permute-start(bf16[96,640]{1,0:T(8,128)(2,1)S(1)} %constant_dynamic-update-slice_fusion.refs_1_), channel_id=1, source_target_pairs={{0,16},{1,17},{2,18},{3,19},{4,20},{5,21},{6,22},{7,23},{8,24},{9,... | collective-permute-start | bytes 368648 | tf_op jit(solution)/shard_map/ppermute | solution.py:88
  14.4 4.9 %collective-permute-start.6 = (bf16[96,640]{1,0:T(8,128)(2,1)S(1)}, bf16[96,640]{1,0:T(8,128)(2,1)S(1)}, u32[]{:S(2)}, u32[]{:S(2)}) collective-permute-start(bf16[96,640]{1,0:T(8,128)(2,1)S(1)} %constant_dynamic-update-slice_fusion.refs_1_), channel_id=1, source_target_pairs={{0,2},{1,3},{2,0},{3,1},{4,6},{5,7},{6,4},{7,5},{8,10},{9,11},{10,... | collective-permute-start | bytes 368648 | tf_op jit(solution)/shard_map/ppermute | solution.py:88
  15.1 4.7 %collective-permute-start.9 = (bf16[128,640]{1,0:T(8,128)(2,1)S(1)}, bf16[128,640]{1,0:T(8,128)(2,1)S(1)}, u32[]{:S(2)}, u32[]{:S(2)}) collective-permute-start(bf16[128,640]{1,0:T(8,128)(2,1)S(1)} %pad_maximum_fusion.refs_0_), channel_id=1, source_target_pairs={{0,1},{1,0},{2,3},{3,2},{4,5},{5,4},{6,7},{7,6},{8,9},{9,8},{10,11... | collective-permute-start | bytes 491528 | tf_op jit(solution)/shard_map/ppermute | solution.py:88
  15.1 4.7 %collective-permute-start.10 = (bf16[96,640]{1,0:T(8,128)(2,1)S(1)}, bf16[96,640]{1,0:T(8,128)(2,1)S(1)}, u32[]{:S(2)}, u32[]{:S(2)}) collective-permute-start(bf16[96,640]{1,0:T(8,128)(2,1)S(1)} %constant_dynamic-update-slice_fusion.refs_1_), channel_id=1, source_target_pairs={{0,1},{1,0},{2,3},{3,2},{4,5},{5,4},{6,7},{7,6},{8,9},{9,8},{10,11... | collective-permute-start | bytes 368648 | tf_op jit(solution)/shard_map/ppermute | solution.py:88
  18.5 1.3 %collective-permute-start.13 = (bf16[96,640]{1,0:T(8,128)(2,1)S(1)}, bf16[96,640]{1,0:T(8,128)(2,1)S(1)}, u32[]{:S(2)}, u32[]{:S(2)}) collective-permute-start(bf16[96,640]{1,0:T(8,128)(2,1)S(1)} %collective-permute-done.8.refs_4_), channel_id=1, source_target_pairs={{0,1},{1,0},{2,3},{3,2},{4,5},{5,4},{6,7},{7,6},{8,9},{9,8},{10,11... | collective-permute-start | bytes 368648 | tf_op jit(solution)/shard_map/ppermute | solution.py:88
  19.3 1.3 %collective-permute-start.12 = (bf16[96,640]{1,0:T(8,128)(2,1)S(1)}, bf16[96,640]{1,0:T(8,128)(2,1)S(1)}, u32[]{:S(2)}, u32[]{:S(2)}) collective-permute-start(bf16[96,640]{1,0:T(8,128)(2,1)S(1)} %collective-permute-done.7.refs_3_), channel_id=1, source_target_pairs={{0,1},{1,0},{2,3},{3,2},{4,5},{5,4},{6,7},{7,6},{8,9},{9,8},{10,11... | collective-permute-start | bytes 368648 | tf_op jit(solution)/shard_map/ppermute | solution.py:88
  19.3 1.5 %collective-permute-start.11 = (bf16[96,640]{1,0:T(8,128)(2,1)S(1)}, bf16[96,640]{1,0:T(8,128)(2,1)S(1)}, u32[]{:S(2)}, u32[]{:S(2)}) collective-permute-start(bf16[96,640]{1,0:T(8,128)(2,1)S(1)} %collective-permute-done.6.refs_2_), channel_id=1, source_target_pairs={{0,1},{1,0},{2,3},{3,2},{4,5},{5,4},{6,7},{7,6},{8,9},{9,8},{10,11... | collective-permute-start | bytes 368648 | tf_op jit(solution)/shard_map/ppermute | solution.py:88
